TPU v7x, 256 devices: a whole 4x4x8 slice. The times are simulated.
256 devices in a mesh: inner: 32 (over y, z_hi, core), outer: 8 (over z_lo, x).
Axes of the slice: x: 4, y: 4, z: 8 (z_hi: 4, z_lo: 2; z = z_hi * 2 + z_lo), core: 2. Of those that a mesh axis runs over, the one named last changes fastest.
Arguments:
- tokens: bfloat16 [65536, 8192], P(('inner', 'outer')), may hold values from -24 to 24
- grad_out: bfloat16 [65536, 8192], P(('inner', 'outer')), may hold values from -0.09375 to 0.09375
- gate_rows: bfloat16 [104, 8192], replicated, may hold values from -0.0625 to 0.0625
- up_rows: bfloat16 [104, 8192], replicated, may hold values from -0.0625 to 0.0625
- down_rows: bfloat16 [104, 8192], replicated, may hold values from -0.0390625 to 0.0390625
Outputs:
- grad_blocks: float32 [3, 3328, 256], P(None, ('inner', 'outer'))
All inputs are finite; a program needn't handle non-finite values. Where the computation divides by a largest or mean magnitude, that divisor is 1e-20 or more.
Results may differ from a plain program's by a relative error of at most 0.0095.
Values may be sent and summed in bfloat16 or wider, within the bound.
No kernel may reach another device: no remote copies, remote signals or barrier semaphores. Data moves between devices by JAX's collectives and lax.ppermute only.
A program may use at most 128 MiB of HBM per device.

v0:
```python
import jax
import jax.numpy as jnp
from jax import lax
from jax.sharding import PartitionSpec as P

BLOCK = 256


EPS = 1e-06


def as_sent(shard):
    return jax.tree.map(lambda a: a.astype(jnp.bfloat16) if a.dtype == jnp.float32 else a, shard)


def encode(values):
    scale = jnp.max(jnp.abs(values), axis=-1) + EPS
    return ((values / scale[..., None]).astype(jnp.bfloat16), scale)


def decode(codes, scales):
    return codes.astype(jnp.float32) * scales[..., None]


def sum_codes_one(pieces):
    return jnp.sum(decode(pieces[0], pieces[1]), axis=1)


def sum_partials_one(piece):
    return jnp.sum(piece, axis=1)


def contract_rows(left, right):
    return lax.dot_general(
        left, right, (((0,), (0,)), ((), ())), preferred_element_type=jnp.float32
    )


def project(rows, weights):
    return lax.dot_general(
        rows, weights, (((1,), (1,)), ((), ())), preferred_element_type=jnp.float32
    )


def per_device(tokens, grad_out, gate_rows, up_rows, down_rows):
    blocks = gate_rows.shape[0] * gate_rows.shape[1] // BLOCK
    n_inner = lax.axis_size("inner")
    n_outer = lax.axis_size("outer")
    share = blocks // (n_inner * n_outer)
    gate = project(tokens, gate_rows)
    up = project(tokens, up_rows)
    sig = jax.nn.sigmoid(gate)
    act = gate * sig
    hidden = (act * up).astype(jnp.bfloat16)
    dh = project(grad_out, down_rows)
    dgate = (dh * up * sig * (1.0 + gate * (1.0 - sig))).astype(jnp.bfloat16)
    dup = (dh * act).astype(jnp.bfloat16)
    g_down = contract_rows(hidden, grad_out)
    g_gate = contract_rows(dgate, tokens)
    g_up = contract_rows(dup, tokens)
    stacked = jnp.stack([g_down, g_gate, g_up]).reshape(3, blocks, BLOCK)
    codes, scales = encode(stacked)
    codes = codes.reshape(3, n_inner, n_outer * share, BLOCK)
    scales = scales.reshape(3, n_inner, n_outer * share)
    partial_sum = sum_codes_one(
        (
            lax.all_to_all(codes, "inner", split_axis=1, concat_axis=1, tiled=True),
            lax.all_to_all(
                scales.astype(jnp.bfloat16), "inner", split_axis=1, concat_axis=1, tiled=True
            ).astype(scales.dtype),
        )
    )
    partial_sum = partial_sum.reshape(3, n_outer, share, BLOCK)
    return sum_partials_one(
        lax.all_to_all(
            as_sent(partial_sum), "outer", split_axis=1, concat_axis=1, tiled=True
        ).astype(partial_sum.dtype)
    )


def solution(mesh):
    in_specs = (P(("inner", "outer"), None), P(("inner", "outer"), None), P(), P(), P())
    out_specs = P(None, ("inner", "outer"), None)
    return jax.shard_map(
        per_device, mesh=mesh, in_specs=in_specs, out_specs=out_specs, check_vma=False
    )
```

profile of v0, /device:TPU:2, one launch (start us, length us, event | category | flops | bytes accessed | tf_op | source)
XLA Modules:
  0.0 213.9 jit_solution(5564228216413400205)
XLA Ops:
  0.0 0.0 copy-start
  0.0 0.0 copy-start.1
  0.0 0.0 copy-start.3
  0.0 1.4 copy-done
  1.5 4.3 %fusion.12 = f32[256,104]{0,1:T(8,128)S(1)} fusion(bf16[256,8192]{1,0:T(8,128)(2,1)} %param.5, bf16[104,8192]{1,0:T(8,128)(2,1)S(1)} %copy-done), kind=kOutput, calls=%fused_computation.19 | convolution fusion | flops 436207616 | bytes 6004736 | tf_op jit(solution)/shard_map/dot_general | solution.py:40
  5.7 0.0 copy-done.1
  5.7 0.0 copy-done.3
  5.7 0.0 copy-start.2
  5.8 0.0 copy-start.4
  5.8 1.5 fusion.13
  7.3 0.7 copy-done.2
  7.9 0.5 copy-done.4
  8.5 1.5 fusion.14
  10.0 2.5 %fusion.5 = f32[104,8192]{1,0:T(8,128)} fusion(bf16[256,8192]{1,0:T(8,128)(2,1)S(1)} %copy-done.1, f32[256,104]{0,1:T(8,128)S(1)} %fusion.14, f32[256,104]{0,1:T(8,128)S(1)} %fusion.12), kind=kOutput, calls=%fused_computation.13 | convolution fusion | flops 436367360 | bytes 7815168 | tf_op jit(solution)/shard_map/dot_general | solution.py:34
  12.5 2.6 %fusion.4 = f32[104,8192]{1,0:T(8,128)} fusion(bf16[256,8192]{1,0:T(8,128)(2,1)S(1)} %copy-done.1, f32[256,104]{0,1:T(8,128)S(1)} %fusion.12, f32[256,104]{0,1:T(8,128)S(1)} %fusion.14, f32[256,104]{0,1:T(8,128)S(1)} %fusion.13), kind=kOutput, calls=%fused_computation.12 | convolution fusion | flops 436473856 | bytes 7921664 | tf_op jit(solution)/shard_map/dot_general | solution.py:34
  15.1 2.6 %fusion.3 = f32[104,8192]{1,0:T(8,128)} fusion(bf16[256,8192]{1,0:T(8,128)(2,1)S(1)} %copy-done.2, f32[256,104]{0,1:T(8,128)S(1)} %fusion.13, f32[256,104]{0,1:T(8,128)S(1)} %fusion.12), kind=kOutput, calls=%fused_computation.11 | convolution fusion | flops 436367360 | bytes 7815168 | tf_op jit(solution)/shard_map/dot_general | solution.py:34
  17.6 4.7 %stack.24 = f32[1,3328,256]{2,1,0:T(8,128)} reshape(f32[104,8192]{1,0:T(8,128)} %fusion.3) | data formatting | bytes 6815744 | tf_op jit(solution)/shard_map/stack | solution.py:61
  22.3 4.7 %stack.25 = f32[1,3328,256]{2,1,0:T(8,128)} reshape(f32[104,8192]{1,0:T(8,128)} %fusion.4) | data formatting | bytes 6815744 | tf_op jit(solution)/shard_map/stack | solution.py:61
  26.9 4.7 %stack.26 = f32[1,3328,256]{2,1,0:T(8,128)} reshape(f32[104,8192]{1,0:T(8,128)} %fusion.5) | data formatting | bytes 6815744 | tf_op jit(solution)/shard_map/stack | solution.py:61
  31.7 5.6 %fusion.1 = f32[3,3328]{1,0:T(4,128)S(1)} fusion(f32[1,3328,256]{2,1,0:T(8,128)} %stack.26, f32[1,3328,256]{2,1,0:T(8,128)} %stack.25, f32[1,3328,256]{2,1,0:T(8,128)} %stack.24), kind=kLoop, calls=%fused_computation.3 | loop fusion | flops 10213632 | bytes 10263552 | tf_op jit(solution)/shard_map/reduce_max | solution.py:17
  37.2 0.1 add.24
  37.4 0.6 copy.14
  38.0 11.5 %all-to-all-start.1 = ((bf16[3,32,104]{2,0,1:T(4,128)(2,1)}), bf16[3,32,104]{2,0,1:T(4,128)(2,1)S(1)}, u32[]{:S(2)}, u32[]{:S(2)}) async-start(bf16[3,32,104]{2,0,1:T(4,128)(2,1)} %copy.14), calls=%async_computation.1 | async-start | bytes 65536 | tf_op jit(solution)/shard_map/all_to_all | solution.py:68
  49.5 4.7 %stack.20 = f32[1,32,104,256]{3,2,1,0:T(8,128)} reshape(f32[104,8192]{1,0:T(8,128)} %fusion.3) | data formatting | bytes 6815744 | tf_op jit(solution)/shard_map/stack | solution.py:61
  54.2 4.7 %stack.21 = f32[1,32,104,256]{3,2,1,0:T(8,128)} reshape(f32[104,8192]{1,0:T(8,128)} %fusion.4) | data formatting | bytes 6815744 | tf_op jit(solution)/shard_map/stack | solution.py:61
  58.9 4.7 %stack.22 = f32[1,32,104,256]{3,2,1,0:T(8,128)} reshape(f32[104,8192]{1,0:T(8,128)} %fusion.5) | data formatting | bytes 6815744 | tf_op jit(solution)/shard_map/stack | solution.py:61
  63.6 7.5 %fusion = bf16[3,32,104,256]{3,2,0,1:T(8,128)(2,1)} fusion(f32[1,32,104,256]{3,2,0,1:T(8,128)} %bitcast.14, f32[1,32,104,256]{3,2,0,1:T(8,128)} %bitcast.13, f32[1,32,104,256]{3,2,0,1:T(8,128)} %bitcast.12, f32[3,32,104]{2,0,1:T(4,128)S(1)} %copy.13), kind=kLoop, calls=%fused_computation.1 | loop fusion | flops 10223616 | bytes 15375360 | tf_op jit(solution)/shard_map/convert_element_type | solution.py:18
  71.1 0.0 all-to-all-done.1
  71.1 9.9 %all-to-all-start = ((bf16[3,32,104,256]{3,2,0,1:T(8,128)(2,1)}), bf16[3,32,104,256]{3,2,0,1:T(8,128)(2,1)}, u32[]{:S(2)}, u32[]{:S(2)}) async-start(bf16[3,32,104,256]{3,2,0,1:T(8,128)(2,1)} %fusion), calls=%async_computation | async-start | bytes 10223616 | tf_op jit(solution)/shard_map/all_to_all | solution.py:67
  81.0 117.7 %all-to-all-done = bf16[3,32,104,256]{3,2,0,1:T(8,128)(2,1)} async-done(((bf16[3,32,104,256]{3,2,0,1:T(8,128)(2,1)}), bf16[3,32,104,256]{3,2,0,1:T(8,128)(2,1)}, u32[]{:S(2)}, u32[]{:S(2)}) %all-to-all-start) | async-done | bytes 5111840 | tf_op jit(solution)/shard_map/all_to_all | solution.py:67
  198.7 4.0 %multiply_reduce_fusion = bf16[3,104,256]{2,1,0:T(8,128)(2,1)S(1)} fusion(bf16[3,32,104,256]{3,2,0,1:T(8,128)(2,1)} %all-to-all-done, f32[3,32,104]{2,0,1:T(4,128)S(1)} %convert_element_type.37), kind=kLoop, calls=%fused_computation.4 | loop fusion | flops 7587840 | bytes 5311488 | tf_op jit(solution)/shard_map/reduce_sum | solution.py:26
  202.7 0.1 convert_element_type.39
  202.8 10.4 %all_to_all.15 = bf16[3,8,13,256]{3,2,0,1:T(8,128)(2,1)S(1)} all-to-all(bf16[3,8,13,256]{3,2,0,1:T(8,128)(2,1)S(1)} %copy.15), channel_id=1, replica_groups=mesh['inner'=32,'outer'=8] {'outer'}, dimensions={1} | all-to-all | bytes 319488 | tf_op jit(solution)/shard_map/all_to_all | solution.py:75
  213.2 0.7 convert_reduce_fusion
  (5 shorter events, 0.1 us)
Async XLA Ops:
  0.0 1.5 copy-start
  0.0 5.7 %copy-start.1 = (bf16[256,8192]{1,0:T(8,128)(2,1)S(1)}, bf16[256,8192]{1,0:T(8,128)(2,1)}, u32[]{:S(2)}) copy-start(bf16[256,8192]{1,0:T(8,128)(2,1)} %param.5) | copy-start | bytes 12582916
  0.0 5.7 %copy-start.3 = (bf16[104,8192]{1,0:T(8,128)(2,1)S(1)}, bf16[104,8192]{1,0:T(8,128)(2,1)}, u32[]{:S(2)}) copy-start(bf16[104,8192]{1,0:T(8,128)(2,1)} %param.8) | copy-start | bytes 5111812
  5.7 2.2 %copy-start.2 = (bf16[256,8192]{1,0:T(8,128)(2,1)S(1)}, bf16[256,8192]{1,0:T(8,128)(2,1)}, u32[]{:S(2)}) copy-start(bf16[256,8192]{1,0:T(8,128)(2,1)} %param.6) | copy-start | bytes 12582916
  5.8 2.7 %copy-start.4 = (bf16[104,8192]{1,0:T(8,128)(2,1)S(1)}, bf16[104,8192]{1,0:T(8,128)(2,1)}, u32[]{:S(2)}) copy-start(bf16[104,8192]{1,0:T(8,128)(2,1)} %param.9) | copy-start | bytes 5111812
  38.0 33.1 %all-to-all-start.1 = ((bf16[3,32,104]{2,0,1:T(4,128)(2,1)}), bf16[3,32,104]{2,0,1:T(4,128)(2,1)S(1)}, u32[]{:S(2)}, u32[]{:S(2)}) async-start(bf16[3,32,104]{2,0,1:T(4,128)(2,1)} %copy.14), calls=%async_computation.1 | async-start | bytes 65536 | tf_op jit(solution)/shard_map/all_to_all | solution.py:68
  71.1 127.6 %all-to-all-start = ((bf16[3,32,104,256]{3,2,0,1:T(8,128)(2,1)}), bf16[3,32,104,256]{3,2,0,1:T(8,128)(2,1)}, u32[]{:S(2)}, u32[]{:S(2)}) async-start(bf16[3,32,104,256]{3,2,0,1:T(8,128)(2,1)} %fusion), calls=%async_computation | async-start | bytes 10223616 | tf_op jit(solution)/shard_map/all_to_all | solution.py:67
where the time goes:
time: 215 us; the launch traced here: 214 us
  waiting for transfers between devices  118 us (55%)
  local copies, waits for them, and re-layouts  31.6 us (15%)
  starting transfers between devices  21.4 us (10%)
  other arithmetic  17.7 us (8%)
  matrix products  14.9 us (7%)
  blocking collectives  10.4 us (5%)
    all_to_all x1, waiting for transfers between devices, per_device(): lax.all_to_all(codes, 'inner', split_axis=1, concat_axis=1, tiled=True)  118 us
    another operation x6, local copies, waits for them, and re-layouts, per_device(): stacked = jnp.stack([g_down, g_gate, g_up]).reshape(3, blocks, BLOCK)  28.1 us
    all_to_all x1, starting transfers between devices, per_device(): lax.all_to_all(scales.astype(jnp.bfloat16), 'inner', split_axis=1, concat...  11.5 us
    all_to_all x1, blocking collectives, per_device(): lax.all_to_all(as_sent(partial_sum), 'outer', split_axis=1, concat_axis=1...  10.4 us
    all_to_all x1, starting transfers between devices, per_device(): lax.all_to_all(codes, 'inner', split_axis=1, concat_axis=1, tiled=True)  9.9 us
    dot_general x3, matrix products, contract_rows(): lax.dot_general(left, right, (((0,), (0,)), ((), ())), preferred_element_...  7.66 us
    convert_element_type x1, other arithmetic, encode(): return ((values / scale[..., None]).astype(jnp.bfloat16), scale)  7.5 us
    dot_general x3, matrix products, project(): lax.dot_general(rows, weights, (((1,), (1,)), ((), ())), preferred_elemen...  7.23 us
  transfers between devices with their start and end apart: 2, of which 1 were waited for; matrix products, arithmetic and copies ran while one was open for 10% of the time, Pallas kernels for 0%

commit v1 on v0

v1 whole, which is shorter than its diff:
```python
import jax
import jax.numpy as jnp
from jax import lax
from jax.experimental import pallas as pl
from jax.experimental.pallas import tpu as pltpu
from jax.sharding import Mesh, PartitionSpec as P

ROWS = 104
D = 8192
BLK = 256
TOK = 256
NCB = D // BLK
OWN = 13
NR0 = 13
QUART = 104
CHUNK = 1024
NCH = D // CHUNK
PACK = 80
AXES = ("y", "zh", "c", "zl", "x")
F32 = jnp.float32
BF16 = jnp.bfloat16
VM = pl.BlockSpec(memory_space=pltpu.VMEM)
HB = pl.BlockSpec(memory_space=pltpu.HBM)
SM = pl.BlockSpec(memory_space=pltpu.SMEM)


def params(mib):
    return pltpu.CompilerParams(vmem_limit_bytes=mib * 1024 * 1024)


def shape(*dims, dtype=BF16):
    return jax.ShapeDtypeStruct(dims, dtype)


def weight_grads(core, a_ref, v_ref, nm, send_ref, own_ref):
    for mine in range(2):

        @pl.when(core == mine)
        def _(mine=mine):
            for cb in range(NCB):
                res = jnp.dot(a_ref[...], v_ref[:, cb * BLK : (cb + 1) * BLK], preferred_element_type=F32)
                for r0 in range(NR0):
                    quarter, off = divmod(NCB * r0 + cb, QUART)
                    out = own_ref if quarter % 2 == mine else send_ref
                    for m in range(nm):
                        lo = m * ROWS + 8 * r0
                        out[m, QUART * (quarter // 2) + off] = res[lo : lo + 8, :].astype(BF16)


def first_kernel(c_ref, x_hbm, g_hbm, wg_hbm, wu_hbm, wd_hbm, send_hbm, own_hbm, h_ref, *scratch):
    x_ref, g_ref, wg_ref, wu_ref, wd_ref, rows, tmp, a_ref, send, own, sems, out_sems = scratch
    copies = []
    pairs = ((x_hbm, x_ref), (wg_hbm, wg_ref), (wu_hbm, wu_ref), (g_hbm, g_ref), (wd_hbm, wd_ref))
    for i in range(NCH):
        cols = pl.ds(i * CHUNK, CHUNK)
        for k, (src, dst) in enumerate(pairs):
            copies.append(pltpu.make_async_copy(src.at[:, cols], dst.at[:, cols], sems.at[k, i]))
            copies[-1].start()

    def project(v, w):
        return lax.dot_general(v, w, (((1,), (1,)), ((), ())), preferred_element_type=F32)

    gate_up = jnp.zeros((TOK, 2 * ROWS), F32)
    back = jnp.zeros((TOK, ROWS), F32)
    for i in range(NCH):
        for k in range(5):
            copies[5 * i + k].wait()
        cols = slice(i * CHUNK, (i + 1) * CHUNK)
        both = jnp.concatenate([wg_ref[:, cols], wu_ref[:, cols]], axis=0)
        gate_up = gate_up + project(x_ref[:, cols], both)
        back = back + project(g_ref[:, cols], wd_ref[:, cols])
    gate_up = gate_up.T
    gate, up, dh = gate_up[:ROWS], gate_up[ROWS:], back.T
    sig = jax.nn.sigmoid(gate)
    act = gate * sig
    terms = (act * up, dh * up * sig * (1.0 + gate * (1.0 - sig)), dh * act)
    for i, term in enumerate(terms):
        for half in range(2):
            lanes = slice(128 * half, 128 * (half + 1))
            rows[i, half] = term[:, lanes]
            for r0 in range(NR0):
                tmp[i, 8 * r0 : 8 * (r0 + 1), lanes] = rows[i, half, pl.ds(r0, 8, stride=NR0), :]
    h_ref[...] = tmp[0].astype(BF16)
    a_ref[...] = jnp.concatenate([tmp[1], tmp[2]], axis=0).astype(BF16)
    weight_grads(c_ref[0], a_ref, x_ref, 2, send, own)
    write_out((send, send_hbm), (own, own_hbm), out_sems)


def write_out(one, two, sems):
    copies = [pltpu.make_async_copy(src, dst, sems.at[i]) for i, (src, dst) in enumerate((one, two))]
    for copy in copies:
        copy.start()
    for copy in copies:
        copy.wait()


def first(core, x, g, wg, wu, wd):
    half = (2, 2 * QUART, 8, BLK)
    return pl.pallas_call(
        first_kernel,
        in_specs=[SM, HB, HB, HB, HB, HB],
        out_specs=[HB, HB, VM],
        out_shape=[shape(*half), shape(*half), shape(ROWS, TOK)],
        scratch_shapes=[
            pltpu.VMEM((TOK, D), BF16),
            pltpu.VMEM((TOK, D), BF16),
            pltpu.VMEM((ROWS, D), BF16),
            pltpu.VMEM((ROWS, D), BF16),
            pltpu.VMEM((ROWS, D), BF16),
            pltpu.VMEM((3, 2, ROWS, 128), F32),
            pltpu.VMEM((3, ROWS, TOK), F32),
            pltpu.VMEM((2 * ROWS, TOK), BF16),
            pltpu.VMEM(half, BF16),
            pltpu.VMEM(half, BF16),
            pltpu.SemaphoreType.DMA((5, NCH)),
            pltpu.SemaphoreType.DMA((2,)),
        ],
        compiler_params=params(60),
        name="first",
    )(core, x, g, wg, wu, wd)


def down_kernel(c_ref, a_ref, g_hbm, send_hbm, own_hbm, g_ref, send, own, sems, out_sems):
    copies = []
    for i in range(NCH):
        cols = pl.ds(i * CHUNK, CHUNK)
        copies.append(pltpu.make_async_copy(g_hbm.at[:, cols], g_ref.at[:, cols], sems.at[i]))
        copies[-1].start()
    for copy in copies:
        copy.wait()
    weight_grads(c_ref[0], a_ref, g_ref, 1, send, own)
    write_out((send, send_hbm), (own, own_hbm), out_sems)


def down(core, a, g):
    half = (1, 2 * QUART, 8, BLK)
    return pl.pallas_call(
        down_kernel,
        in_specs=[SM, VM, HB],
        out_specs=[HB, HB],
        out_shape=[shape(*half), shape(*half)],
        scratch_shapes=[
            pltpu.VMEM((TOK, D), BF16),
            pltpu.VMEM(half, BF16),
            pltpu.VMEM(half, BF16),
            pltpu.SemaphoreType.DMA((NCH,)),
            pltpu.SemaphoreType.DMA((2,)),
        ],
        compiler_params=params(60),
        name="down",
    )(core, a, g)


def add_kernel(o0, g0, o1, g1, out_ref, packed):
    pairs = ((o0, g0, 0), (o1, g1, 0), (o1, g1, 1))
    for d in range(8):
        for t in range(8):
            for half in range(2):
                packed[half, d, PACK * t + 6 * OWN : PACK * (t + 1), :] = jnp.zeros((PACK - 6 * OWN, 128), F32)
        for m, (own, got, i) in enumerate(pairs):
            for low in range(2):
                for off in range(OWN):
                    at = QUART * low + OWN * d + off
                    tile = own[i, at].astype(F32) + got[i, at].astype(F32)
                    lo = OWN * (2 * m + low) + off
                    for half in range(2):
                        packed[half, d, pl.ds(lo, 8, stride=PACK), :] = tile[:, 128 * half : 128 * (half + 1)]
        for y in range(4):
            for half in range(2):
                piece = packed[half, d, 2 * PACK * y : 2 * PACK * (y + 1), :]
                out_ref[8 * y + d, :, 128 * half : 128 * (half + 1)] = piece.astype(BF16)


def add_cores(o0, g0, o1, g1):
    return pl.pallas_call(
        add_kernel,
        in_specs=[VM] * 4,
        out_specs=VM,
        out_shape=shape(32, 2 * PACK, BLK),
        scratch_shapes=[pltpu.VMEM((2, 8, 8 * PACK, 128), F32)],
        compiler_params=params(24),
        name="add_cores",
    )(o0, g0, o1, g1)


def sum_near_kernel(in_ref, out_ref, total, packed):
    total[...] = jnp.sum(in_ref[...].astype(F32), axis=0)
    packed[:, 3 * OWN :, :] = jnp.zeros((4, 1, BLK), F32)
    for high in range(2):
        for low in range(2):
            for m in range(3):
                lo = PACK * high + OWN * (2 * m + low)
                packed[2 * high + low, OWN * m : OWN * (m + 1), :] = total[lo : lo + OWN, :]
    out_ref[...] = packed[...].astype(BF16)


def sum_near(parts):
    return pl.pallas_call(
        sum_near_kernel,
        in_specs=[VM],
        out_specs=VM,
        out_shape=shape(4, 40, BLK),
        scratch_shapes=[pltpu.VMEM((2 * PACK, BLK), F32), pltpu.VMEM((4, 40, BLK), F32)],
        compiler_params=params(8),
        name="sum_near",
    )(parts)


def sum_far_kernel(in_ref, out_ref):
    total = jnp.sum(in_ref[...].astype(F32), axis=0)
    for m in range(3):
        out_ref[m] = total[OWN * m : OWN * (m + 1), :]


def sum_far(parts):
    return pl.pallas_call(
        sum_far_kernel,
        in_specs=[VM],
        out_specs=VM,
        out_shape=shape(3, OWN, BLK, dtype=F32),
        compiler_params=params(8),
        name="sum_far",
    )(parts)


def per_device(tokens, grad_out, gate_rows, up_rows, down_rows):
    core = lax.axis_index("c").astype(jnp.int32).reshape(1)
    swap = [(0, 1), (1, 0)]

    def exchange(parts, axes):
        return lax.all_to_all(parts, axes, split_axis=0, concat_axis=0, tiled=True)

    send1, own1, hid = first(core, tokens, grad_out, gate_rows, up_rows, down_rows)
    got1 = lax.ppermute(send1, "c", swap)
    send0, own0 = down(core, hid, grad_out)
    got0 = lax.ppermute(send0, "c", swap)
    parts = add_cores(own0, got0, own1, got1)
    parts = sum_near(exchange(parts, ("y", "zl", "x")))
    return sum_far(exchange(parts, "zh"))


def solution(mesh):
    fine = Mesh(mesh.devices.reshape(4, 4, 2, 2, 4), AXES)
    tok = P(AXES, None)
    return jax.shard_map(
        per_device,
        mesh=fine,
        in_specs=(tok, tok, P(), P(), P()),
        out_specs=P(None, AXES, None),
        check_vma=False,
    )
```

time: 215 us -> 80.1 us (0.37)
  waiting for transfers between devices: 118 us -> 2.22 us
  blocking collectives: 10.4 us -> 58.3 us
  local copies, waits for them, and re-layouts: 31.6 us -> 1.16 us
  starting transfers between devices: 21.4 us -> 0.66 us
  other arithmetic: 17.7 us -> 0 us
  Pallas kernels: 0 us -> 17.5 us
  matrix products: 14.9 us -> 0 us
    all_to_all x2 -> x0, waiting for transfers between devices: 118 us -> none  [the longest x1 118 us: per_device(): lax.all_to_all(codes, 'inner', split_axis=1, concat_axis=1, tiled=True)]
    all_to_all x1 -> x2, blocking collectives: 10.4 us -> 58.3 us  [exchange(): return lax.all_to_all(parts, axes, split_axis=0, concat_axis=0, tiled=True)]
    another operation x6 -> x0, local copies, waits for them, and re-layouts: 28.1 us -> none  [per_device(): stacked = jnp.stack([g_down, g_gate, g_up]).reshape(3, blocks, BLOCK)]
    all_to_all x2 -> x0, starting transfers between devices: 21.4 us -> none  [the longest x1 11.5 us: per_device(): lax.all_to_all(scales.astype(jnp.bfloat16), 'inner', split_axis=1, concat...]
    pallas_call x0 -> x5, Pallas kernels: none -> 17.5 us  [the longest x1 9.21 us: first(): pl.pallas_call(first_kernel, in_specs=[SM, HB, HB, HB, HB, HB], out_specs...]
    dot_general x6 -> x0, matrix products: 14.9 us -> none  [the longest x3 7.66 us: contract_rows(): lax.dot_general(left, right, (((0,), (0,)), ((), ())), preferred_element_...]
    convert_element_type x3 -> x0, other arithmetic: 7.52 us -> none  [the longest x1 7.5 us: encode(): return ((values / scale[..., None]).astype(jnp.bfloat16), scale)]
    reduce_max x1 -> x0, other arithmetic: 5.56 us -> none  [encode(): scale = jnp.max(jnp.abs(values), axis=-1) + EPS]
  transfers between devices with their start and end apart: 2 -> 2, of which waited for: 1 -> 1; matrix products, arithmetic and copies ran while one was open for 10% -> 0% of each run, Pallas kernels for 0% -> 6%
where the time goes in v1:
time: 80.1 us; the launch traced here: 79.9 us
  blocking collectives  58.3 us (73%)
  Pallas kernels  17.5 us (22%)
  waiting for transfers between devices  2.22 us (3%)
  local copies, waits for them, and re-layouts  1.16 us (1%)
    all_to_all x2, blocking collectives, exchange(): return lax.all_to_all(parts, axes, split_axis=0, concat_axis=0, tiled=True)  58.3 us
    pallas_call x1, Pallas kernels, first(): pl.pallas_call(first_kernel, in_specs=[SM, HB, HB, HB, HB, HB], out_specs...  9.21 us
    pallas_call x1, Pallas kernels, down(): pl.pallas_call(down_kernel, in_specs=[SM, VM, HB], out_specs=[HB, HB], ou...  5.19 us
    ppermute x1, waiting for transfers between devices, per_device(): got0 = lax.ppermute(send0, 'c', swap)  2.22 us
    pallas_call x1, Pallas kernels, add_cores(): pl.pallas_call(add_kernel, in_specs=[VM] * 4, out_specs=VM, out_shape=sha...  1.96 us
  transfers between devices with their start and end apart: 2, of which 1 were waited for; matrix products, arithmetic and copies ran while one was open for 0% of the time, Pallas kernels for 6%

profile of v1, /device:TPU:2, one launch (start us, length us, event | category | flops | bytes accessed | tf_op | source)
XLA Modules:
  0.0 79.9 jit_solution(14615472470436198150)
XLA Ops:
  0.0 9.2 %first.1 = (bf16[2,208,8,256]{3,2,1,0:T(8,128)(2,1)}, bf16[2,208,8,256]{3,2,1,0:T(8,128)(2,1)}, bf16[104,256]{1,0:T(8,128)(2,1)}) custom-call(s32[1]{0:T(128)} %bitcast.c_ref, bf16[256,8192]{1,0:T(8,128)(2,1)} %x_hbm.1, bf16[256,8192]{1,0:T(8,128)(2,1)} %g_hbm.3, bf16[104,8192]{1,0:T(8,128)(2,1)} %wg_hbm.1, bf16[104,8192]{1,0:T(8,128)(2,1)} %wu_hbm.1, ...), custom_call_target="tpu_custom_call" | custom-call | tf_op jit(solution)/shard_map/first/pallas_call | solution.py:99
  9.2 0.1 collective-permute-start.1
  9.3 0.0 copy-start
  9.3 5.2 %down.1 = (bf16[1,208,8,256]{3,2,1,0:T(8,128)(2,1)}, bf16[1,208,8,256]{3,2,1,0:T(8,128)(2,1)}) custom-call(s32[1]{0:T(128)} %bitcast.c_ref, bf16[104,256]{1,0:T(8,128)(2,1)} %get-tuple-element.10.a_ref, bf16[256,8192]{1,0:T(8,128)(2,1)} %g_hbm.3), custom_call_target="tpu_custom_call" | custom-call | tf_op jit(solution)/shard_map/down/pallas_call | solution.py:137
  14.5 0.6 collective-permute-start
  15.1 2.2 %collective-permute-done.g0 = bf16[1,208,8,256]{3,2,1,0:T(8,128)(2,1)S(1)} collective-permute-done((bf16[1,208,8,256]{3,2,1,0:T(8,128)(2,1)}, bf16[1,208,8,256]{3,2,1,0:T(8,128)(2,1)S(1)}, u32[]{:S(2)}, u32[]{:S(2)}) %collective-permute-start) | collective-permute-done | bytes 852000 | tf_op jit(solution)/shard_map/ppermute | solution.py:236
  17.3 0.0 collective-permute-done.1.g1
  17.3 0.0 copy-done
  17.3 0.0 copy-start.1
  17.3 1.2 %copy-done.1 = bf16[1,208,8,256]{3,2,1,0:T(8,128)(2,1)S(1)} copy-done((bf16[1,208,8,256]{3,2,1,0:T(8,128)(2,1)S(1)}, bf16[1,208,8,256]{3,2,1,0:T(8,128)(2,1)}, u32[]{:S(2)}) %copy-start.1) | copy-done | bytes 851992
  18.5 2.0 %add_cores.1 = bf16[32,160,256]{2,1,0:T(8,128)(2,1)S(1)} custom-call(bf16[1,208,8,256]{3,2,1,0:T(8,128)(2,1)S(1)} %copy-done.1, bf16[1,208,8,256]{3,2,1,0:T(8,128)(2,1)S(1)} %collective-permute-done.g0, bf16[2,208,8,256]{3,2,1,0:T(8,128)(2,1)S(1)} %copy-done, bf16[2,208,8,256]{3,2,1,0:T(8,128)(2,1)S(1)} %collective-permute-done.1.g1), custom_call_target="tpu_custom_call" | custom-call | tf_op jit(solution)/shard_map/add_cores/pallas_call | solution.py:175
  20.4 42.6 %all_to_all.10.in_ref = bf16[32,160,256]{2,1,0:T(8,128)(2,1)S(1)} all-to-all(bf16[32,160,256]{2,1,0:T(8,128)(2,1)S(1)} %add_cores.1), channel_id=1, replica_groups=mesh['y'=4,'zh'=4,'c'=2,'zl'=2,'x'=4] {'y','zl','x'}, dimensions={0} | all-to-all | bytes 5242880 | tf_op jit(solution)/shard_map/all_to_all | solution.py:231
  63.0 0.5 sum_near.1
  63.6 15.7 %all_to_all.11.in_ref = bf16[4,40,256]{2,1,0:T(8,128)(2,1)S(1)} all-to-all(bf16[4,40,256]{2,1,0:T(8,128)(2,1)S(1)} %sum_near.1), channel_id=1, replica_groups=mesh['y'=4,'zh'=4,'c'=2,'zl'=2,'x'=4] {'zh'}, dimensions={0} | all-to-all | bytes 163840 | tf_op jit(solution)/shard_map/all_to_all | solution.py:231
  79.3 0.6 sum_far.1
Async XLA Ops:
  9.2 8.1 %collective-permute-start.1 = (bf16[2,208,8,256]{3,2,1,0:T(8,128)(2,1)}, bf16[2,208,8,256]{3,2,1,0:T(8,128)(2,1)S(1)}, u32[]{:S(2)}, u32[]{:S(2)}) collective-permute-start(bf16[2,208,8,256]{3,2,1,0:T(8,128)(2,1)} %get-tuple-element.14), channel_id=1, source_target_pairs={{0,8},{8,0},{1,9},{9,1},{2,10},{10,2},{3,11},{11,3},{4,12},{12,4},... | collective-permute-start | bytes 5111816 | tf_op jit(solution)/shard_map/ppermute | solution.py:234
  9.3 8.0 %copy-start = (bf16[2,208,8,256]{3,2,1,0:T(8,128)(2,1)S(1)}, bf16[2,208,8,256]{3,2,1,0:T(8,128)(2,1)}, u32[]{:S(2)}) copy-start(bf16[2,208,8,256]{3,2,1,0:T(8,128)(2,1)} %get-tuple-element.13.o1) | copy-start | bytes 5111812
  14.5 2.8 %collective-permute-start = (bf16[1,208,8,256]{3,2,1,0:T(8,128)(2,1)}, bf16[1,208,8,256]{3,2,1,0:T(8,128)(2,1)S(1)}, u32[]{:S(2)}, u32[]{:S(2)}) collective-permute-start(bf16[1,208,8,256]{3,2,1,0:T(8,128)(2,1)} %get-tuple-element.12), channel_id=1, source_target_pairs={{0,8},{8,0},{1,9},{9,1},{2,10},{10,2},{3,11},{11,3},{4,12},{12,4},... | collective-permute-start | bytes 2555912 | tf_op jit(solution)/shard_map/ppermute | solution.py:236
  17.3 1.2 %copy-start.1 = (bf16[1,208,8,256]{3,2,1,0:T(8,128)(2,1)S(1)}, bf16[1,208,8,256]{3,2,1,0:T(8,128)(2,1)}, u32[]{:S(2)}) copy-start(bf16[1,208,8,256]{3,2,1,0:T(8,128)(2,1)} %get-tuple-element.11.o0) | copy-start | bytes 2555908

commit v2 on v1

v2 whole, which is shorter than its diff:
```python
import jax
import jax.numpy as jnp
from jax import lax
from jax.experimental import pallas as pl
from jax.experimental.pallas import tpu as pltpu
from jax.sharding import Mesh, PartitionSpec as P

ROWS = 104
D = 8192
BLK = 256
TOK = 256
NCB = D // BLK
OWN = 13
NR0 = 13
QUART = 104
CUTS = tuple(range(0, D + 1, 1024))
AXES = ("y", "zh", "c", "zl", "x")
TERMS_MIB = 40
F32 = jnp.float32
BF16 = jnp.bfloat16
VM = pl.BlockSpec(memory_space=pltpu.VMEM)
HB = pl.BlockSpec(memory_space=pltpu.HBM)
SM = pl.BlockSpec(memory_space=pltpu.SMEM)


def params(mib):
    return pltpu.CompilerParams(vmem_limit_bytes=mib * 1024 * 1024)


def shape(*dims, dtype=BF16):
    return jax.ShapeDtypeStruct(dims, dtype)


def permuted(term, rows, out, i):
    for half in range(2):
        lanes = slice(128 * half, 128 * (half + 1))
        rows[i, half] = term[:, lanes]
        for r0 in range(NR0):
            out[i, 8 * r0 : 8 * (r0 + 1), lanes] = rows[i, half, pl.ds(r0, 8, stride=NR0), :]


def weight_grads(mine, a_ref, v_ref, send, own, first, count):
    for cb in range(NCB):
        res = jnp.dot(a_ref[...], v_ref[:, cb * BLK : (cb + 1) * BLK], preferred_element_type=F32)
        for r0 in range(NR0):
            quarter, off = divmod(NCB * r0 + cb, QUART)
            out = own if quarter % 2 == mine else send
            for m in range(count):
                lo = m * ROWS + 8 * r0
                out[first + m, QUART * (quarter // 2) + off] = res[lo : lo + 8, :].astype(BF16)


def fetch(pairs, sems):
    copies = []
    for i, (lo, hi) in enumerate(zip(CUTS, CUTS[1:])):
        cols = pl.ds(lo, hi - lo)
        copies.append([pltpu.make_async_copy(s.at[:, cols], d.at[:, cols], sems.at[k, i]) for k, (s, d) in enumerate(pairs)])
        for copy in copies[-1]:
            copy.start()
    return copies


def terms_kernel(c_ref, x_hbm, g_hbm, wg_hbm, wu_hbm, wd_hbm, send, own, *scratch):
    x_ref, g_ref, wg_ref, wu_ref, wd_ref, rows, tmp, a0_ref, a12_ref, sems = scratch
    pairs = ((x_hbm, x_ref), (wg_hbm, wg_ref), (wu_hbm, wu_ref), (g_hbm, g_ref), (wd_hbm, wd_ref))
    fetched = fetch(pairs, sems)

    def project(v, w):
        return lax.dot_general(v, w, (((1,), (1,)), ((), ())), preferred_element_type=F32)

    gate_up = jnp.zeros((TOK, 2 * ROWS), F32)
    dh = jnp.zeros((TOK, ROWS), F32)
    for copies, lo, hi in zip(fetched, CUTS, CUTS[1:]):
        for copy in copies:
            copy.wait()
        cols = slice(lo, hi)
        both = jnp.concatenate([wg_ref[:, cols], wu_ref[:, cols]], axis=0)
        gate_up = gate_up + project(x_ref[:, cols], both)
        dh = dh + project(g_ref[:, cols], wd_ref[:, cols])
    gate_up = gate_up.T
    gate, up, dh = gate_up[:ROWS], gate_up[ROWS:], dh.T
    sig = jax.nn.sigmoid(gate)
    act = gate * sig
    permuted(act * up, rows, tmp, 0)
    permuted(dh * up * sig * (1.0 + gate * (1.0 - sig)), rows, tmp, 1)
    permuted(dh * act, rows, tmp, 2)
    a0_ref[...] = tmp[0].astype(BF16)
    a12_ref[...] = jnp.concatenate([tmp[1], tmp[2]], axis=0).astype(BF16)
    for mine in range(2):

        @pl.when(c_ref[0] == mine)
        def _(mine=mine):
            weight_grads(mine, a0_ref, g_ref, send, own, 0, 1)
            weight_grads(mine, a12_ref, x_ref, send, own, 1, 2)


def terms(core, *inputs):
    half = pltpu.VMEM((3, 2 * QUART, 8, BLK), BF16)
    inputs = [pltpu.with_memory_space_constraint(a, pltpu.HBM) for a in inputs]
    return pl.pallas_call(
        terms_kernel,
        in_specs=[SM, HB, HB, HB, HB, HB],
        out_specs=[VM, VM],
        out_shape=[half, half],
        scratch_shapes=[
            pltpu.VMEM((TOK, D), BF16),
            pltpu.VMEM((TOK, D), BF16),
            pltpu.VMEM((ROWS, D), BF16),
            pltpu.VMEM((ROWS, D), BF16),
            pltpu.VMEM((ROWS, D), BF16),
            pltpu.VMEM((3, 2, ROWS, 128), F32),
            pltpu.VMEM((3, ROWS, TOK), F32),
            pltpu.VMEM((ROWS, TOK), BF16),
            pltpu.VMEM((2 * ROWS, TOK), BF16),
            pltpu.SemaphoreType.DMA((5, len(CUTS) - 1)),
        ],
        compiler_params=params(TERMS_MIB),
        name="terms",
    )(core, *inputs)


def add_kernel(own, got, out_ref, packed):
    for d in range(8):
        for m in range(3):
            for low in range(2):
                for off in range(OWN):
                    at = QUART * low + OWN * d + off
                    tile = own[m, at].astype(F32) + got[m, at].astype(F32)
                    for half in range(2):
                        lo = OWN * (6 * half + 2 * m + low) + off
                        packed[d, pl.ds(lo, 8, stride=12 * OWN), :] = tile[:, 128 * half : 128 * (half + 1)]
        for y in range(4):
            out_ref[8 * y + d] = packed[d, 24 * OWN * y : 24 * OWN * (y + 1), :].astype(BF16)


def add_cores(own, got):
    return pl.pallas_call(
        add_kernel,
        in_specs=[VM] * 2,
        out_specs=VM,
        out_shape=shape(32, 24 * OWN, 128),
        scratch_shapes=[pltpu.VMEM((8, 8 * 12 * OWN, 128), F32)],
        compiler_params=params(16),
        name="add_cores",
    )(own, got)


def sum_near_kernel(in_ref, out_ref, total, packed):
    total[...] = jnp.sum(in_ref[...].astype(F32), axis=0)
    packed[:, 6 * OWN :, :] = jnp.zeros((4, 2, 128), F32)
    for high in range(2):
        for low in range(2):
            for half in range(2):
                for m in range(3):
                    src = OWN * (12 * high + 6 * half + 2 * m + low)
                    dst = OWN * (3 * half + m)
                    packed[2 * high + low, dst : dst + OWN, :] = total[src : src + OWN, :]
    out_ref[...] = packed[...].astype(BF16)


def sum_near(parts):
    return pl.pallas_call(
        sum_near_kernel,
        in_specs=[VM],
        out_specs=VM,
        out_shape=shape(4, 80, 128),
        scratch_shapes=[pltpu.VMEM((24 * OWN, 128), F32), pltpu.VMEM((4, 80, 128), F32)],
        compiler_params=params(8),
        name="sum_near",
    )(parts)


def sum_far_kernel(in_ref, out_ref):
    total = jnp.sum(in_ref[...].astype(F32), axis=0)
    for half in range(2):
        for m in range(3):
            lo = OWN * (3 * half + m)
            out_ref[m, :, 128 * half : 128 * (half + 1)] = total[lo : lo + OWN, :]


def sum_far(parts):
    return pl.pallas_call(
        sum_far_kernel,
        in_specs=[VM],
        out_specs=VM,
        out_shape=shape(3, OWN, BLK, dtype=F32),
        compiler_params=params(8),
        name="sum_far",
    )(parts)


def per_device(tokens, grad_out, gate_rows, up_rows, down_rows):
    core = lax.axis_index("c").astype(jnp.int32).reshape(1)
    swap = [(0, 1), (1, 0)]

    def exchange(parts, axes):
        return lax.all_to_all(parts, axes, split_axis=0, concat_axis=0, tiled=True)

    send, own = terms(core, tokens, grad_out, gate_rows, up_rows, down_rows)
    parts = add_cores(own, lax.ppermute(send, "c", swap))
    parts = sum_near(exchange(parts, ("y", "zl", "x")))
    return sum_far(exchange(parts, "zh"))


def solution(mesh):
    fine = Mesh(mesh.devices.reshape(4, 4, 2, 2, 4), AXES)
    tok = P(AXES, None)
    return jax.shard_map(
        per_device,
        mesh=fine,
        in_specs=(tok, tok, P(), P(), P()),
        out_specs=P(None, AXES, None),
        check_vma=False,
    )
```

time: 80.1 us -> 71.7 us (0.90)
  Pallas kernels: 17.5 us -> 9.28 us
  waiting for transfers between devices: 2.22 us -> 4.8 us
  local copies, waits for them, and re-layouts: 1.16 us -> 0 us
  blocking collectives: 58.3 us -> 57.3 us
    pallas_call x3 -> x2, Pallas kernels: 16.4 us -> 8.15 us  [the longest x1 7.44 us: terms(): pl.pallas_call(terms_kernel, in_specs=[SM, HB, HB, HB, HB, HB], out_specs...]
    ppermute x2 -> x1, waiting for transfers between devices: 2.22 us -> 4.8 us  [per_device(): parts = add_cores(own, lax.ppermute(send, 'c', swap))]
    unnamed x4 -> x0, local copies, waits for them, and re-layouts: 1.16 us -> none
    all_to_all x2, blocking collectives: 58.3 us -> 57.3 us  [exchange(): return lax.all_to_all(parts, axes, split_axis=0, concat_axis=0, tiled=True)]
  transfers between devices with their start and end apart: 2 -> 1, of which waited for: 1 -> 1; matrix products, arithmetic and copies ran while one was open for 0% -> 0% of each run, Pallas kernels for 6% -> 0%
where the time goes in v2:
time: 71.7 us; the launch traced here: 71.5 us
  blocking collectives  57.3 us (80%)
  Pallas kernels  9.28 us (13%)
  waiting for transfers between devices  4.8 us (7%)
    all_to_all x2, blocking collectives, exchange(): return lax.all_to_all(parts, axes, split_axis=0, concat_axis=0, tiled=True)  57.3 us
    pallas_call x1, Pallas kernels, terms(): pl.pallas_call(terms_kernel, in_specs=[SM, HB, HB, HB, HB, HB], out_specs...  7.44 us
    ppermute x1, waiting for transfers between devices, per_device(): parts = add_cores(own, lax.ppermute(send, 'c', swap))  4.8 us
  transfers between devices with their start and end apart: 1, of which 1 were waited for; matrix products, arithmetic and copies ran while one was open for 0% of the time, Pallas kernels for 0%

profile of v2, /device:TPU:2, one launch (start us, length us, event | category | flops | bytes accessed | tf_op | source)
XLA Modules:
  0.0 71.5 jit_solution(13762923898302295830)
XLA Ops:
  0.0 7.4 %terms.1 = (bf16[3,208,8,256]{3,2,1,0:T(8,128)(2,1)S(1)}, bf16[3,208,8,256]{3,2,1,0:T(8,128)(2,1)S(1)}) custom-call(s32[1]{0:T(128)} %bitcast.c_ref, bf16[256,8192]{1,0:T(8,128)(2,1)} %x_hbm.1, bf16[256,8192]{1,0:T(8,128)(2,1)} %g_hbm.1, bf16[104,8192]{1,0:T(8,128)(2,1)} %wg_hbm.1, bf16[104,8192]{1,0:T(8,128)(2,1)} %wu_hbm.1, bf16[104,8192]{1,0:T(8,128)(2,1)} %wd_hbm.1), custom_call_target="tpu_custom_call" | custom-call | tf_op jit(solution)/shard_map/terms/pallas_call | solution.py:100
  7.4 0.1 collective-permute-start
  7.5 4.8 %collective-permute-done.got = bf16[3,208,8,256]{3,2,1,0:T(8,128)(2,1)S(1)} collective-permute-done((bf16[3,208,8,256]{3,2,1,0:T(8,128)(2,1)S(1)}, bf16[3,208,8,256]{3,2,1,0:T(8,128)(2,1)S(1)}, u32[]{:S(2)}, u32[]{:S(2)}) %collective-permute-start) | collective-permute-done | bytes 2555936 | tf_op jit(solution)/shard_map/ppermute | solution.py:200
  12.4 0.7 add_cores.1
  13.1 41.6 %all_to_all.10.in_ref = bf16[32,312,128]{2,1,0:T(8,128)(2,1)S(1)} all-to-all(bf16[32,312,128]{2,1,0:T(8,128)(2,1)S(1)} %add_cores.1), channel_id=1, replica_groups=mesh['y'=4,'zh'=4,'c'=2,'zl'=2,'x'=4] {'y','zl','x'}, dimensions={0} | all-to-all | bytes 5111808 | tf_op jit(solution)/shard_map/all_to_all | solution.py:197
  54.7 0.5 sum_near.1
  55.2 15.7 %all_to_all.11.in_ref = bf16[4,80,128]{2,1,0:T(8,128)(2,1)S(1)} all-to-all(bf16[4,80,128]{2,1,0:T(8,128)(2,1)S(1)} %sum_near.1), channel_id=1, replica_groups=mesh['y'=4,'zh'=4,'c'=2,'zl'=2,'x'=4] {'zh'}, dimensions={0} | all-to-all | bytes 163840 | tf_op jit(solution)/shard_map/all_to_all | solution.py:197
  70.9 0.6 sum_far.1
Async XLA Ops:
  7.4 4.9 %collective-permute-start = (bf16[3,208,8,256]{3,2,1,0:T(8,128)(2,1)S(1)}, bf16[3,208,8,256]{3,2,1,0:T(8,128)(2,1)S(1)}, u32[]{:S(2)}, u32[]{:S(2)}) collective-permute-start(bf16[3,208,8,256]{3,2,1,0:T(8,128)(2,1)S(1)} %get-tuple-element.8), channel_id=1, source_target_pairs={{0,8},{8,0},{1,9},{9,1},{2,10},{10,2},{3,11},{11,3},{4,12},{12,4},... | collective-permute-start | bytes 7667720 | tf_op jit(solution)/shard_map/ppermute | solution.py:200

commit v3 on v2

--- a/solution.py
+++ b/solution.py
@@ -1,3 +1,5 @@
+import functools
+
 import jax
 import jax.numpy as jnp
 from jax import lax
@@ -15,12 +17,12 @@
 QUART = 104
 CUTS = tuple(range(0, D + 1, 1024))
 AXES = ("y", "zh", "c", "zl", "x")
+PAD = 160
 TERMS_MIB = 40
 F32 = jnp.float32
 BF16 = jnp.bfloat16
 VM = pl.BlockSpec(memory_space=pltpu.VMEM)
 HB = pl.BlockSpec(memory_space=pltpu.HBM)
-SM = pl.BlockSpec(memory_space=pltpu.SMEM)
 
 
 def params(mib):
@@ -39,15 +41,14 @@
             out[i, 8 * r0 : 8 * (r0 + 1), lanes] = rows[i, half, pl.ds(r0, 8, stride=NR0), :]
 
 
-def weight_grads(mine, a_ref, v_ref, send, own, first, count):
+def weight_grads(mine, a_ref, v_ref, sends, owns):
     for cb in range(NCB):
         res = jnp.dot(a_ref[...], v_ref[:, cb * BLK : (cb + 1) * BLK], preferred_element_type=F32)
         for r0 in range(NR0):
             quarter, off = divmod(NCB * r0 + cb, QUART)
-            out = own if quarter % 2 == mine else send
-            for m in range(count):
+            for m, out in enumerate(owns if quarter % 2 == mine else sends):
                 lo = m * ROWS + 8 * r0
-                out[first + m, QUART * (quarter // 2) + off] = res[lo : lo + 8, :].astype(BF16)
+                out[QUART * (quarter // 2) + off] = res[lo : lo + 8, :].astype(BF16)
 
 
 def fetch(pairs, sems):
@@ -60,7 +61,8 @@
     return copies
 
 
-def terms_kernel(c_ref, x_hbm, g_hbm, wg_hbm, wu_hbm, wd_hbm, send, own, *scratch):
+def terms_kernel(x_hbm, g_hbm, wg_hbm, wu_hbm, wd_hbm, *rest):
+    sends, owns, scratch = rest[0:3], rest[3:6], rest[6:]
     x_ref, g_ref, wg_ref, wu_ref, wd_ref, rows, tmp, a0_ref, a12_ref, sems = scratch
     pairs = ((x_hbm, x_ref), (wg_hbm, wg_ref), (wu_hbm, wu_ref), (g_hbm, g_ref), (wd_hbm, wd_ref))
     fetched = fetch(pairs, sems)
@@ -88,20 +90,20 @@
     a12_ref[...] = jnp.concatenate([tmp[1], tmp[2]], axis=0).astype(BF16)
     for mine in range(2):
 
-        @pl.when(c_ref[0] == mine)
+        @pl.when(lax.axis_index("c") == mine)
         def _(mine=mine):
-            weight_grads(mine, a0_ref, g_ref, send, own, 0, 1)
-            weight_grads(mine, a12_ref, x_ref, send, own, 1, 2)
-
-
-def terms(core, *inputs):
-    half = pltpu.VMEM((3, 2 * QUART, 8, BLK), BF16)
+            weight_grads(mine, a0_ref, g_ref, sends[:1], owns[:1])
+            weight_grads(mine, a12_ref, x_ref, sends[1:], owns[1:])
+
+
+def terms(*inputs):
+    half = pltpu.VMEM((2 * QUART, 8, BLK), BF16)
     inputs = [pltpu.with_memory_space_constraint(a, pltpu.HBM) for a in inputs]
     return pl.pallas_call(
         terms_kernel,
-        in_specs=[SM, HB, HB, HB, HB, HB],
-        out_specs=[VM, VM],
-        out_shape=[half, half],
+        in_specs=[HB] * 5,
+        out_specs=[VM] * 6,
+        out_shape=[half] * 6,
         scratch_shapes=[
             pltpu.VMEM((TOK, D), BF16),
             pltpu.VMEM((TOK, D), BF16),
@@ -116,45 +118,89 @@
         ],
         compiler_params=params(TERMS_MIB),
         name="terms",
-    )(core, *inputs)
-
-
-def add_kernel(own, got, out_ref, packed):
+    )(*inputs)
+
+
+def pair_place(axis):
+    at = lax.axis_index(axis)
+    return at if axis == "zl" else (at >> lax.axis_index("c")) & 1
+
+
+def add_kernel(axis, own, got, keep, give, halves):
     for d in range(8):
-        for m in range(3):
-            for low in range(2):
-                for off in range(OWN):
-                    at = QUART * low + OWN * d + off
-                    tile = own[m, at].astype(F32) + got[m, at].astype(F32)
-                    for half in range(2):
-                        lo = OWN * (6 * half + 2 * m + low) + off
-                        packed[d, pl.ds(lo, 8, stride=12 * OWN), :] = tile[:, 128 * half : 128 * (half + 1)]
-        for y in range(4):
-            out_ref[8 * y + d] = packed[d, 24 * OWN * y : 24 * OWN * (y + 1), :].astype(BF16)
-
-
-def add_cores(own, got):
-    return pl.pallas_call(
-        add_kernel,
+        for low in range(2):
+            for off in range(OWN):
+                at = QUART * low + OWN * d + off
+                tile = own[at].astype(F32) + got[at].astype(F32)
+                for half in range(2):
+                    lo = OWN * low + off
+                    halves[half, d, pl.ds(lo, 8, stride=2 * OWN), :] = tile[:, 128 * half : 128 * (half + 1)]
+    mine = pair_place(axis)
+    keep[...] = halves[mine].astype(BF16)
+    give[...] = halves[1 - mine].astype(BF16)
+
+
+def add_cores(axis, own, got):
+    return pl.pallas_call(
+        functools.partial(add_kernel, axis),
         in_specs=[VM] * 2,
+        out_specs=[VM] * 2,
+        out_shape=[shape(8, 16 * OWN, 128)] * 2,
+        scratch_shapes=[pltpu.VMEM((2, 8, 16 * OWN, 128), F32)],
+        compiler_params=params(16),
+        name="add_" + axis,
+    )(own, got)
+
+
+def add_pair_kernel(k0, k1, k2, g0, g1, g2, out_ref, total, packed):
+    n = 4 * OWN
+    packed[:, 3 * n :, :] = jnp.zeros((32, PAD - 3 * n, 128), F32)
+    for m, (keep, got) in enumerate(((k0, g0), (k1, g1), (k2, g2))):
+        total[...] = keep[...].astype(F32) + got[...].astype(F32)
+        for d in range(8):
+            for y in range(4):
+                packed[8 * y + d, n * m : n * (m + 1), :] = total[d, n * y : n * (y + 1), :]
+    out_ref[...] = packed[...].astype(BF16)
+
+
+def add_pair(*parts):
+    return pl.pallas_call(
+        add_pair_kernel,
+        in_specs=[VM] * 6,
         out_specs=VM,
-        out_shape=shape(32, 24 * OWN, 128),
-        scratch_shapes=[pltpu.VMEM((8, 8 * 12 * OWN, 128), F32)],
+        out_shape=shape(32, PAD, 128),
+        scratch_shapes=[pltpu.VMEM((8, 16 * OWN, 128), F32), pltpu.VMEM((32, PAD, 128), F32)],
         compiler_params=params(16),
-        name="add_cores",
-    )(own, got)
+        name="add_pair",
+    )(*parts)
 
 
 def sum_near_kernel(in_ref, out_ref, total, packed):
-    total[...] = jnp.sum(in_ref[...].astype(F32), axis=0)
+    def add(sources, m):
+        lo, hi = 4 * OWN * m, 4 * OWN * (m + 1)
+        value = in_ref[sources[0], lo:hi, :].astype(F32)
+        for source in sources[1:]:
+            value = value + in_ref[source, lo:hi, :].astype(F32)
+        return value
+
+    for core in range(2):
+
+        @pl.when(lax.axis_index("c") == core)
+        def _(core=core):
+            for half in range(2):
+                total[0, half] = add([s for s in range(32) if (s % 4 >> core) & 1 == half], 0)
+                total[1, half] = add([s for s in range(32) if (s // 8 >> core) & 1 == half], 1)
+
+    for half in range(2):
+        total[2, half] = add([s for s in range(32) if s // 4 % 2 == half], 2)
     packed[:, 6 * OWN :, :] = jnp.zeros((4, 2, 128), F32)
     for high in range(2):
         for low in range(2):
             for half in range(2):
                 for m in range(3):
-                    src = OWN * (12 * high + 6 * half + 2 * m + low)
+                    src = OWN * (2 * high + low)
                     dst = OWN * (3 * half + m)
-                    packed[2 * high + low, dst : dst + OWN, :] = total[src : src + OWN, :]
+                    packed[2 * high + low, dst : dst + OWN, :] = total[m, half, src : src + OWN, :]
     out_ref[...] = packed[...].astype(BF16)
 
 
@@ -164,7 +210,7 @@
         in_specs=[VM],
         out_specs=VM,
         out_shape=shape(4, 80, 128),
-        scratch_shapes=[pltpu.VMEM((24 * OWN, 128), F32), pltpu.VMEM((4, 80, 128), F32)],
+        scratch_shapes=[pltpu.VMEM((3, 2, 4 * OWN, 128), F32), pltpu.VMEM((4, 80, 128), F32)],
         compiler_params=params(8),
         name="sum_near",
     )(parts)
@@ -190,16 +236,28 @@
 
 
 def per_device(tokens, grad_out, gate_rows, up_rows, down_rows):
-    core = lax.axis_index("c").astype(jnp.int32).reshape(1)
-    swap = [(0, 1), (1, 0)]
-
     def exchange(parts, axes):
         return lax.all_to_all(parts, axes, split_axis=0, concat_axis=0, tiled=True)
 
-    send, own = terms(core, tokens, grad_out, gate_rows, up_rows, down_rows)
-    parts = add_cores(own, lax.ppermute(send, "c", swap))
-    parts = sum_near(exchange(parts, ("y", "zl", "x")))
+    ring = [(i ^ 1, 3 - i) for i in range(4)]
+    long = [(i ^ 1, (i + 1 if i % 2 else i - 1) % 8) for i in range(8)]
+    pairs = (
+        (("c", "x"), [(4 * c + i, 4 * c + ring[i][c]) for c in range(2) for i in range(4)]),
+        (("y", "c"), [(2 * i + c, 2 * ring[i][c] + c) for c in range(2) for i in range(4)]),
+        (("zh", "c", "zl"), [(place(i, c), place(long[i][c], c)) for c in range(2) for i in range(8)]),
+    )
+    sends_owns = terms(tokens, grad_out, gate_rows, up_rows, down_rows)
+    keeps, gots = [], []
+    for axis, send, own, (axes, perm) in zip(("x", "y", "zl"), sends_owns[:3], sends_owns[3:], pairs, strict=True):
+        keep, give = add_cores(axis, own, lax.ppermute(send, "c", [(0, 1), (1, 0)]))
+        keeps.append(keep)
+        gots.append(lax.ppermute(give, axes, perm))
+    parts = sum_near(exchange(add_pair(*keeps, *gots), ("y", "zl", "x")))
     return sum_far(exchange(parts, "zh"))
+
+
+def place(z, c):
+    return 4 * (z // 2) + 2 * c + z % 2
 
 
 def solution(mesh):

time: 71.7 us -> 66.2 us (0.923)
  blocking collectives: 57.3 us -> 43.1 us
  starting transfers between devices: 0.09 us -> 5.3 us
  waiting for transfers between devices: 4.8 us -> 7.98 us
    all_to_all x2, blocking collectives: 57.3 us -> 43.1 us  [exchange(): return lax.all_to_all(parts, axes, split_axis=0, concat_axis=0, tiled=True)]
    ppermute x1 -> x6, starting transfers between devices: 0.09 us -> 5.3 us  [the longest x3 4.61 us: per_device(): gots.append(lax.ppermute(give, axes, perm))]
    ppermute x1 -> x6, waiting for transfers between devices: 4.8 us -> 7.98 us  [the longest x3 6.2 us: per_device(): gots.append(lax.ppermute(give, axes, perm))]
    pallas_call x2 -> x5, Pallas kernels: 8.15 us -> 8.77 us  [the longest x1 7.44 us: terms(): pl.pallas_call(terms_kernel, in_specs=[HB] * 5, out_specs=[VM] * 6, out_s...]
  transfers between devices with their start and end apart: 1 -> 6, of which waited for: 1 -> 4; matrix products, arithmetic and copies ran while one was open for 0% -> 0% of each run, Pallas kernels for 0% -> 1%
where the time goes in v3:
time: 66.2 us; the launch traced here: 66 us
  blocking collectives  43.1 us (65%)
  Pallas kernels  9.61 us (15%)
  waiting for transfers between devices  7.98 us (12%)
  starting transfers between devices  5.3 us (8%)
    all_to_all x2, blocking collectives, exchange(): return lax.all_to_all(parts, axes, split_axis=0, concat_axis=0, tiled=True)  43.1 us
    pallas_call x1, Pallas kernels, terms(): pl.pallas_call(terms_kernel, in_specs=[HB] * 5, out_specs=[VM] * 6, out_s...  7.44 us
    ppermute x3, waiting for transfers between devices, per_device(): gots.append(lax.ppermute(give, axes, perm))  6.2 us
    ppermute x3, starting transfers between devices, per_device(): gots.append(lax.ppermute(give, axes, perm))  4.61 us
    ppermute x3, waiting for transfers between devices, per_device(): keep, give = add_cores(axis, own, lax.ppermute(send, 'c', [(0, 1), (1, 0)]))  1.77 us
  transfers between devices with their start and end apart: 6, of which 4 were waited for; matrix products, arithmetic and copies ran while one was open for 0% of the time, Pallas kernels for 1%

profile of v3, /device:TPU:2, one launch (start us, length us, event | category | flops | bytes accessed | tf_op | source)
XLA Modules:
  0.0 66.0 jit_solution(5701253093511408411)
XLA Ops:
  0.0 7.4 %terms.1 = (bf16[208,8,256]{2,1,0:T(8,128)(2,1)S(1)}, bf16[208,8,256]{2,1,0:T(8,128)(2,1)S(1)}, bf16[208,8,256]{2,1,0:T(8,128)(2,1)S(1)}, bf16[208,8,256]{2,1,0:...) custom-call(bf16[256,8192]{1,0:T(8,128)(2,1)} %x_hbm.1, bf16[256,8192]{1,0:T(8,128)(2,1)} %g_hbm.1, ...), custom_call_target="tpu_custom_call" | custom-call | tf_op jit(solution)/shard_map/terms/pallas_call | solution.py:102
  7.4 0.1 collective-permute-start
  7.5 0.5 collective-permute-start.1
  8.0 0.1 collective-permute-start.2
  8.1 1.8 %collective-permute-done.got = bf16[208,8,256]{2,1,0:T(8,128)(2,1)S(1)} collective-permute-done((bf16[208,8,256]{2,1,0:T(8,128)(2,1)S(1)}, bf16[208,8,256]{2,1,0:T(8,128)(2,1)S(1)}, u32[]{:S(2)}, u32[]{:S(2)}) %collective-permute-start) | collective-permute-done | bytes 852000 | tf_op jit(solution)/shard_map/ppermute | solution.py:252
  9.9 0.3 add_x.1
  10.2 2.4 %collective-permute-start.3 = (bf16[8,208,128]{2,1,0:T(8,128)(2,1)S(1)}, bf16[8,208,128]{2,1,0:T(8,128)(2,1)S(1)}, u32[]{:S(2)}, u32[]{:S(2)}) collective-permute-start(bf16[8,208,128]{2,1,0:T(8,128)(2,1)S(1)} %get-tuple-element.26), channel_id=1, source_target_pairs={{0,1},{1,0},{2,3},{3,2},{8,11},{9,10},{10,9},{11,8},{4,5},{5,4},{6... | collective-permute-start | bytes 1277960 | tf_op jit(solution)/shard_map/ppermute | solution.py:254
  12.5 0.0 collective-permute-done.1.got
  12.5 0.3 add_y.1
  12.8 0.3 collective-permute-start.4
  13.1 0.0 collective-permute-done.2.got
  13.1 0.3 add_zl.1
  13.3 2.0 %collective-permute-start.5 = (bf16[8,208,128]{2,1,0:T(8,128)(2,1)S(1)}, bf16[8,208,128]{2,1,0:T(8,128)(2,1)S(1)}, u32[]{:S(2)}, u32[]{:S(2)}) collective-permute-start(bf16[8,208,128]{2,1,0:T(8,128)(2,1)S(1)} %get-tuple-element.28), channel_id=1, source_target_pairs={{0,4},{4,0},{16,20},{20,16},{32,36},{36,32},{48,52},{52,48},{8,60}... | collective-permute-start | bytes 1277960 | tf_op jit(solution)/shard_map/ppermute | solution.py:254
  15.3 3.3 %collective-permute-done.3.g0 = bf16[8,208,128]{2,1,0:T(8,128)(2,1)S(1)} collective-permute-done((bf16[8,208,128]{2,1,0:T(8,128)(2,1)S(1)}, bf16[8,208,128]{2,1,0:T(8,128)(2,1)S(1)}, u32[]{:S(2)}, u32[]{:S(2)}) %collective-permute-start.3) | collective-permute-done | bytes 426016 | tf_op jit(solution)/shard_map/ppermute | solution.py:254
  18.6 2.4 %collective-permute-done.4.g1 = bf16[8,208,128]{2,1,0:T(8,128)(2,1)S(1)} collective-permute-done((bf16[8,208,128]{2,1,0:T(8,128)(2,1)S(1)}, bf16[8,208,128]{2,1,0:T(8,128)(2,1)S(1)}, u32[]{:S(2)}, u32[]{:S(2)}) %collective-permute-start.4) | collective-permute-done | bytes 426016 | tf_op jit(solution)/shard_map/ppermute | solution.py:254
  21.0 0.5 collective-permute-done.5.g2
  21.5 0.5 add_pair.1
  22.1 29.4 %all_to_all.10.in_ref = bf16[32,160,128]{2,1,0:T(8,128)(2,1)S(1)} all-to-all(bf16[32,160,128]{2,1,0:T(8,128)(2,1)S(1)} %add_pair.1), channel_id=1, replica_groups=mesh['y'=4,'zh'=4,'c'=2,'zl'=2,'x'=4] {'y','zl','x'}, dimensions={0} | all-to-all | bytes 2621440 | tf_op jit(solution)/shard_map/all_to_all | solution.py:240
  51.5 0.2 sum_near.1
  51.7 13.6 %all_to_all.11.in_ref = bf16[4,80,128]{2,1,0:T(8,128)(2,1)S(1)} all-to-all(bf16[4,80,128]{2,1,0:T(8,128)(2,1)S(1)} %sum_near.1), channel_id=1, replica_groups=mesh['y'=4,'zh'=4,'c'=2,'zl'=2,'x'=4] {'zh'}, dimensions={0} | all-to-all | bytes 163840 | tf_op jit(solution)/shard_map/all_to_all | solution.py:240
  65.4 0.6 sum_far.1
Async XLA Ops:
  7.4 2.5 %collective-permute-start = (bf16[208,8,256]{2,1,0:T(8,128)(2,1)S(1)}, bf16[208,8,256]{2,1,0:T(8,128)(2,1)S(1)}, u32[]{:S(2)}, u32[]{:S(2)}) collective-permute-start(bf16[208,8,256]{2,1,0:T(8,128)(2,1)S(1)} %get-tuple-element.18), channel_id=1, source_target_pairs={{0,8},{8,0},{1,9},{9,1},{2,10},{10,2},{3,11},{11,3},{4,12},{12,4},... | collective-permute-start | bytes 2555912 | tf_op jit(solution)/shard_map/ppermute | solution.py:252
  7.5 5.0 %collective-permute-start.1 = (bf16[208,8,256]{2,1,0:T(8,128)(2,1)S(1)}, bf16[208,8,256]{2,1,0:T(8,128)(2,1)S(1)}, u32[]{:S(2)}, u32[]{:S(2)}) collective-permute-start(bf16[208,8,256]{2,1,0:T(8,128)(2,1)S(1)} %get-tuple-element.21), channel_id=1, source_target_pairs={{0,8},{8,0},{1,9},{9,1},{2,10},{10,2},{3,11},{11,3},{4,12},{12,4},... | collective-permute-start | bytes 2555912 | tf_op jit(solution)/shard_map/ppermute | solution.py:252
  8.0 5.0 %collective-permute-start.2 = (bf16[208,8,256]{2,1,0:T(8,128)(2,1)S(1)}, bf16[208,8,256]{2,1,0:T(8,128)(2,1)S(1)}, u32[]{:S(2)}, u32[]{:S(2)}) collective-permute-start(bf16[208,8,256]{2,1,0:T(8,128)(2,1)S(1)} %get-tuple-element.24), channel_id=1, source_target_pairs={{0,8},{8,0},{1,9},{9,1},{2,10},{10,2},{3,11},{11,3},{4,12},{12,4},... | collective-permute-start | bytes 2555912 | tf_op jit(solution)/shard_map/ppermute | solution.py:252
  10.2 8.5 %collective-permute-start.3 = (bf16[8,208,128]{2,1,0:T(8,128)(2,1)S(1)}, bf16[8,208,128]{2,1,0:T(8,128)(2,1)S(1)}, u32[]{:S(2)}, u32[]{:S(2)}) collective-permute-start(bf16[8,208,128]{2,1,0:T(8,128)(2,1)S(1)} %get-tuple-element.26), channel_id=1, source_target_pairs={{0,1},{1,0},{2,3},{3,2},{8,11},{9,10},{10,9},{11,8},{4,5},{5,4},{6... | collective-permute-start | bytes 1277960 | tf_op jit(solution)/shard_map/ppermute | solution.py:254
  12.8 8.2 %collective-permute-start.4 = (bf16[8,208,128]{2,1,0:T(8,128)(2,1)S(1)}, bf16[8,208,128]{2,1,0:T(8,128)(2,1)S(1)}, u32[]{:S(2)}, u32[]{:S(2)}) collective-permute-start(bf16[8,208,128]{2,1,0:T(8,128)(2,1)S(1)} %get-tuple-element.27), channel_id=1, source_target_pairs={{0,64},{64,0},{128,192},{192,128},{8,200},{72,136},{136,72},{200,8... | collective-permute-start | bytes 1277960 | tf_op jit(solution)/shard_map/ppermute | solution.py:254
  13.3 8.2 %collective-permute-start.5 = (bf16[8,208,128]{2,1,0:T(8,128)(2,1)S(1)}, bf16[8,208,128]{2,1,0:T(8,128)(2,1)S(1)}, u32[]{:S(2)}, u32[]{:S(2)}) collective-permute-start(bf16[8,208,128]{2,1,0:T(8,128)(2,1)S(1)} %get-tuple-element.28), channel_id=1, source_target_pairs={{0,4},{4,0},{16,20},{20,16},{32,36},{36,32},{48,52},{52,48},{8,60}... | collective-permute-start | bytes 1277960 | tf_op jit(solution)/shard_map/ppermute | solution.py:254

commit v4 on v3

--- a/solution.py
+++ b/solution.py
@@ -17,7 +17,8 @@
 QUART = 104
 CUTS = tuple(range(0, D + 1, 1024))
 AXES = ("y", "zh", "c", "zl", "x")
-PAD = 160
+ORDER = "zxy"
+PAD = 80
 TERMS_MIB = 40
 F32 = jnp.float32
 BF16 = jnp.bfloat16
@@ -121,9 +122,14 @@
     )(*inputs)
 
 
-def pair_place(axis):
-    at = lax.axis_index(axis)
-    return at if axis == "zl" else (at >> lax.axis_index("c")) & 1
+def pair_place(axis, level):
+    c = lax.axis_index("c")
+    if axis == "z":
+        low = lax.axis_index("zl")
+        return low if level else ((2 * lax.axis_index("zh") + low + 1 - c) >> 1) & 1
+    i = lax.axis_index(axis)
+    high, low = i >> 1, i & 1
+    return jnp.where(c == 0, high, low) if level else high ^ ((1 - c) * low)
 
 
 def add_kernel(axis, own, got, keep, give, halves):
@@ -133,9 +139,8 @@
                 at = QUART * low + OWN * d + off
                 tile = own[at].astype(F32) + got[at].astype(F32)
                 for half in range(2):
-                    lo = OWN * low + off
-                    halves[half, d, pl.ds(lo, 8, stride=2 * OWN), :] = tile[:, 128 * half : 128 * (half + 1)]
-    mine = pair_place(axis)
+                    halves[half, low, d, pl.ds(off, 8, stride=OWN), :] = tile[:, 128 * half : 128 * (half + 1)]
+    mine = pair_place(axis, 0)
     keep[...] = halves[mine].astype(BF16)
     give[...] = halves[1 - mine].astype(BF16)
 
@@ -145,15 +150,32 @@
         functools.partial(add_kernel, axis),
         in_specs=[VM] * 2,
         out_specs=[VM] * 2,
-        out_shape=[shape(8, 16 * OWN, 128)] * 2,
-        scratch_shapes=[pltpu.VMEM((2, 8, 16 * OWN, 128), F32)],
+        out_shape=[shape(2, 8, 8 * OWN, 128)] * 2,
+        scratch_shapes=[pltpu.VMEM((2, 2, 8, 8 * OWN, 128), F32)],
         compiler_params=params(16),
         name="add_" + axis,
     )(own, got)
 
 
-def add_pair_kernel(k0, k1, k2, g0, g1, g2, out_ref, total, packed):
-    n = 4 * OWN
+def add_pair_kernel(axis, mine, got, keep, give):
+    at = pair_place(axis, 1)
+    for out, low in ((keep, at), (give, 1 - at)):
+        out[...] = (mine[low].astype(F32) + got[low].astype(F32)).astype(BF16)
+
+
+def add_pair(axis, mine, got):
+    return pl.pallas_call(
+        functools.partial(add_pair_kernel, axis),
+        in_specs=[VM] * 2,
+        out_specs=[VM] * 2,
+        out_shape=[shape(8, 8 * OWN, 128)] * 2,
+        compiler_params=params(16),
+        name="add_pair_" + axis,
+    )(mine, got)
+
+
+def add_four_kernel(k0, k1, k2, g0, g1, g2, out_ref, total, packed):
+    n = 2 * OWN
     packed[:, 3 * n :, :] = jnp.zeros((32, PAD - 3 * n, 128), F32)
     for m, (keep, got) in enumerate(((k0, g0), (k1, g1), (k2, g2))):
         total[...] = keep[...].astype(F32) + got[...].astype(F32)
@@ -163,44 +185,49 @@
     out_ref[...] = packed[...].astype(BF16)
 
 
-def add_pair(*parts):
-    return pl.pallas_call(
-        add_pair_kernel,
+def add_four(*parts):
+    return pl.pallas_call(
+        add_four_kernel,
         in_specs=[VM] * 6,
         out_specs=VM,
         out_shape=shape(32, PAD, 128),
-        scratch_shapes=[pltpu.VMEM((8, 16 * OWN, 128), F32), pltpu.VMEM((32, PAD, 128), F32)],
+        scratch_shapes=[pltpu.VMEM((8, 8 * OWN, 128), F32), pltpu.VMEM((32, PAD, 128), F32)],
         compiler_params=params(16),
-        name="add_pair",
+        name="add_four",
     )(*parts)
 
 
 def sum_near_kernel(in_ref, out_ref, total, packed):
+    n = 2 * OWN
+
     def add(sources, m):
-        lo, hi = 4 * OWN * m, 4 * OWN * (m + 1)
-        value = in_ref[sources[0], lo:hi, :].astype(F32)
+        value = in_ref[sources[0], n * m : n * (m + 1), :].astype(F32)
         for source in sources[1:]:
-            value = value + in_ref[source, lo:hi, :].astype(F32)
+            value = value + in_ref[source, n * m : n * (m + 1), :].astype(F32)
         return value
 
+    mx, my, mz = (ORDER.index(axis) for axis in "xyz")
     for core in range(2):
 
         @pl.when(lax.axis_index("c") == core)
         def _(core=core):
-            for half in range(2):
-                total[0, half] = add([s for s in range(32) if (s % 4 >> core) & 1 == half], 0)
-                total[1, half] = add([s for s in range(32) if (s // 8 >> core) & 1 == half], 1)
-
-    for half in range(2):
-        total[2, half] = add([s for s in range(32) if s // 4 % 2 == half], 2)
+            for i in range(4):
+                high, low = i >> 1, i & 1
+                half, part = (high, low) if core else (high ^ low, high)
+                total[mx, half, part] = add([s for s in range(32) if s % 4 == i], mx)
+                total[my, half, part] = add([s for s in range(32) if s // 8 == i], my)
+
+    total[mz] = jnp.zeros((2, 2, n, 128), F32)
+    for low in range(2):
+        half = ((2 * lax.axis_index("zh") + low + 1 - lax.axis_index("c")) >> 1) & 1
+        total[mz, half, low] = add([s for s in range(32) if s // 4 % 2 == low], mz)
     packed[:, 6 * OWN :, :] = jnp.zeros((4, 2, 128), F32)
     for high in range(2):
         for low in range(2):
             for half in range(2):
                 for m in range(3):
-                    src = OWN * (2 * high + low)
                     dst = OWN * (3 * half + m)
-                    packed[2 * high + low, dst : dst + OWN, :] = total[m, half, src : src + OWN, :]
+                    packed[2 * high + low, dst : dst + OWN, :] = total[m, half, low, OWN * high : OWN * (high + 1), :]
     out_ref[...] = packed[...].astype(BF16)
 
 
@@ -210,7 +237,7 @@
         in_specs=[VM],
         out_specs=VM,
         out_shape=shape(4, 80, 128),
-        scratch_shapes=[pltpu.VMEM((3, 2, 4 * OWN, 128), F32), pltpu.VMEM((4, 80, 128), F32)],
+        scratch_shapes=[pltpu.VMEM((3, 2, 2, 2 * OWN, 128), F32), pltpu.VMEM((4, 80, 128), F32)],
         compiler_params=params(8),
         name="sum_near",
     )(parts)
@@ -239,20 +266,27 @@
     def exchange(parts, axes):
         return lax.all_to_all(parts, axes, split_axis=0, concat_axis=0, tiled=True)
 
-    ring = [(i ^ 1, 3 - i) for i in range(4)]
+    near = [(i ^ 1, 3 - i) for i in range(4)]
     long = [(i ^ 1, (i + 1 if i % 2 else i - 1) % 8) for i in range(8)]
-    pairs = (
-        (("c", "x"), [(4 * c + i, 4 * c + ring[i][c]) for c in range(2) for i in range(4)]),
-        (("y", "c"), [(2 * i + c, 2 * ring[i][c] + c) for c in range(2) for i in range(4)]),
-        (("zh", "c", "zl"), [(place(i, c), place(long[i][c], c)) for c in range(2) for i in range(8)]),
-    )
+
+    def pairs(level):
+        cores = [(c, c ^ level) for c in range(2)]
+        return {
+            "x": (("c", "x"), [(4 * c + i, 4 * c + near[i][k]) for c, k in cores for i in range(4)]),
+            "y": (("y", "c"), [(2 * i + c, 2 * near[i][k] + c) for c, k in cores for i in range(4)]),
+            "z": (("zh", "c", "zl"), [(place(i, c), place(long[i][k], c)) for c, k in cores for i in range(8)]),
+        }
+
     sends_owns = terms(tokens, grad_out, gate_rows, up_rows, down_rows)
     keeps, gots = [], []
-    for axis, send, own, (axes, perm) in zip(("x", "y", "zl"), sends_owns[:3], sends_owns[3:], pairs, strict=True):
-        keep, give = add_cores(axis, own, lax.ppermute(send, "c", [(0, 1), (1, 0)]))
+    for axis, send, own in zip(ORDER, sends_owns[:3], sends_owns[3:], strict=True):
+        parts = add_cores(axis, own, lax.ppermute(send, "c", [(0, 1), (1, 0)]))
+        for level in range(2):
+            keep, give = parts if level == 0 else add_pair(axis, keep, got)
+            got = lax.ppermute(give, *pairs(level)[axis])
         keeps.append(keep)
-        gots.append(lax.ppermute(give, axes, perm))
-    parts = sum_near(exchange(add_pair(*keeps, *gots), ("y", "zl", "x")))
+        gots.append(got)
+    parts = sum_near(exchange(add_four(*keeps, *gots), ("y", "zl", "x")))
     return sum_far(exchange(parts, "zh"))
 
 

time: 66.2 us -> 64.2 us (0.970)
  blocking collectives: 43.1 us -> 29.6 us
  starting transfers between devices: 5.3 us -> 15.6 us
  waiting for transfers between devices: 7.98 us -> 9.22 us
    all_to_all x2, blocking collectives: 43.1 us -> 29.6 us  [exchange(): return lax.all_to_all(parts, axes, split_axis=0, concat_axis=0, tiled=True)]
    ppermute x6 -> x9, starting transfers between devices: 5.3 us -> 15.6 us  [the longest x6 14.9 us: per_device(): got = lax.ppermute(give, *pairs(level)[axis])]
    ppermute x6 -> x9, waiting for transfers between devices: 7.98 us -> 9.22 us  [the longest x6 7.45 us: per_device(): got = lax.ppermute(give, *pairs(level)[axis])]
  transfers between devices with their start and end apart: 6 -> 9, of which waited for: 4 -> 4; matrix products, arithmetic and copies ran while one was open for 0% -> 0% of each run, Pallas kernels for 1% -> 2%
where the time goes in v4:
time: 64.2 us; the launch traced here: 64 us
  blocking collectives  29.6 us (46%)
  starting transfers between devices  15.6 us (24%)
  Pallas kernels  9.56 us (15%)
  waiting for transfers between devices  9.22 us (14%)
    all_to_all x2, blocking collectives, exchange(): return lax.all_to_all(parts, axes, split_axis=0, concat_axis=0, tiled=True)  29.6 us
    ppermute x6, starting transfers between devices, per_device(): got = lax.ppermute(give, *pairs(level)[axis])  14.9 us
    ppermute x6, waiting for transfers between devices, per_device(): got = lax.ppermute(give, *pairs(level)[axis])  7.45 us
    pallas_call x1, Pallas kernels, terms(): pl.pallas_call(terms_kernel, in_specs=[HB] * 5, out_specs=[VM] * 6, out_s...  7.44 us
    ppermute x3, waiting for transfers between devices, per_device(): parts = add_cores(axis, own, lax.ppermute(send, 'c', [(0, 1), (1, 0)]))  1.77 us
  transfers between devices with their start and end apart: 9, of which 4 were waited for; matrix products, arithmetic and copies ran while one was open for 0% of the time, Pallas kernels for 2%

profile of v4, /device:TPU:2, one launch (start us, length us, event | category | flops | bytes accessed | tf_op | source)
XLA Modules:
  0.0 64.0 jit_solution(15102223554862800286)
XLA Ops:
  0.0 7.4 %terms.1 = (bf16[208,8,256]{2,1,0:T(8,128)(2,1)S(1)}, bf16[208,8,256]{2,1,0:T(8,128)(2,1)S(1)}, bf16[208,8,256]{2,1,0:T(8,128)(2,1)S(1)}, bf16[208,8,256]{2,1,0:...) custom-call(bf16[256,8192]{1,0:T(8,128)(2,1)} %x_hbm.1, bf16[256,8192]{1,0:T(8,128)(2,1)} %g_hbm.1, ...), custom_call_target="tpu_custom_call" | custom-call | tf_op jit(solution)/shard_map/terms/pallas_call | solution.py:103
  7.4 0.1 collective-permute-start
  7.5 0.5 collective-permute-start.2
  8.0 0.1 collective-permute-start.4
  8.1 1.8 %collective-permute-done.got = bf16[208,8,256]{2,1,0:T(8,128)(2,1)S(1)} collective-permute-done((bf16[208,8,256]{2,1,0:T(8,128)(2,1)S(1)}, bf16[208,8,256]{2,1,0:T(8,128)(2,1)S(1)}, u32[]{:S(2)}, u32[]{:S(2)}) %collective-permute-start) | collective-permute-done | bytes 852000 | tf_op jit(solution)/shard_map/ppermute | solution.py:283
  9.9 0.3 add_z.1
  10.2 2.0 %collective-permute-start.1 = (bf16[2,8,104,128]{3,2,1,0:T(8,128)(2,1)S(1)}, bf16[2,8,104,128]{3,2,1,0:T(8,128)(2,1)S(1)}, u32[]{:S(2)}, u32[]{:S(2)}) collective-permute-start(bf16[2,8,104,128]{3,2,1,0:T(8,128)(2,1)S(1)} %get-tuple-element.26), channel_id=1, source_target_pairs={{0,4},{4,0},{16,20},{20,16},{32,36},{36,32},{48,52},{52,48},{8,60}... | collective-permute-start | bytes 1277960 | tf_op jit(solution)/shard_map/ppermute | solution.py:286
  12.2 0.0 collective-permute-done.2.got
  12.2 0.3 add_x.1
  12.4 1.3 %collective-permute-start.3 = (bf16[2,8,104,128]{3,2,1,0:T(8,128)(2,1)S(1)}, bf16[2,8,104,128]{3,2,1,0:T(8,128)(2,1)S(1)}, u32[]{:S(2)}, u32[]{:S(2)}) collective-permute-start(bf16[2,8,104,128]{3,2,1,0:T(8,128)(2,1)S(1)} %get-tuple-element.31), channel_id=1, source_target_pairs={{0,1},{1,0},{2,3},{3,2},{8,11},{9,10},{10,9},{11,8},{4,5},{5,4},{6... | collective-permute-start | bytes 1277960 | tf_op jit(solution)/shard_map/ppermute | solution.py:286
  13.7 0.0 collective-permute-done.4.got
  13.7 0.3 add_y.1
  14.0 1.0 %collective-permute-start.5 = (bf16[2,8,104,128]{3,2,1,0:T(8,128)(2,1)S(1)}, bf16[2,8,104,128]{3,2,1,0:T(8,128)(2,1)S(1)}, u32[]{:S(2)}, u32[]{:S(2)}) collective-permute-start(bf16[2,8,104,128]{3,2,1,0:T(8,128)(2,1)S(1)} %get-tuple-element.36), channel_id=1, source_target_pairs={{0,64},{64,0},{128,192},{192,128},{8,200},{72,136},{136,72},{200,8... | collective-permute-start | bytes 1277960 | tf_op jit(solution)/shard_map/ppermute | solution.py:286
  15.0 3.4 %collective-permute-done.1.got = bf16[2,8,104,128]{3,2,1,0:T(8,128)(2,1)S(1)} collective-permute-done((bf16[2,8,104,128]{3,2,1,0:T(8,128)(2,1)S(1)}, bf16[2,8,104,128]{3,2,1,0:T(8,128)(2,1)S(1)}, u32[]{:S(2)}, u32[]{:S(2)}) %collective-permute-start.1) | collective-permute-done | bytes 426016 | tf_op jit(solution)/shard_map/ppermute | solution.py:286
  18.4 0.1 add_pair_z.1
  18.5 5.9 %collective-permute-start.6 = (bf16[8,104,128]{2,1,0:T(8,128)(2,1)S(1)}, bf16[8,104,128]{2,1,0:T(8,128)(2,1)S(1)}, u32[]{:S(2)}, u32[]{:S(2)}) collective-permute-start(bf16[8,104,128]{2,1,0:T(8,128)(2,1)S(1)} %get-tuple-element.38), channel_id=1, source_target_pairs={{0,52},{4,16},{16,4},{20,32},{32,20},{36,48},{48,36},{52,0},{8,12}... | collective-permute-start | bytes 638984 | tf_op jit(solution)/shard_map/ppermute | solution.py:286
  24.4 0.0 collective-permute-done.3.got
  24.4 0.1 add_pair_x.1
  24.5 1.6 %collective-permute-start.7 = (bf16[8,104,128]{2,1,0:T(8,128)(2,1)S(1)}, bf16[8,104,128]{2,1,0:T(8,128)(2,1)S(1)}, u32[]{:S(2)}, u32[]{:S(2)}) collective-permute-start(bf16[8,104,128]{2,1,0:T(8,128)(2,1)S(1)} %get-tuple-element.39), channel_id=1, source_target_pairs={{0,3},{1,2},{2,1},{3,0},{8,9},{9,8},{10,11},{11,10},{4,7},{5,6},{6... | collective-permute-start | bytes 638984 | tf_op jit(solution)/shard_map/ppermute | solution.py:286
  26.1 0.0 collective-permute-done.5.got
  26.1 0.1 add_pair_y.1
  26.2 3.1 %collective-permute-start.8 = (bf16[8,104,128]{2,1,0:T(8,128)(2,1)S(1)}, bf16[8,104,128]{2,1,0:T(8,128)(2,1)S(1)}, u32[]{:S(2)}, u32[]{:S(2)}) collective-permute-start(bf16[8,104,128]{2,1,0:T(8,128)(2,1)S(1)} %get-tuple-element.40), channel_id=1, source_target_pairs={{0,192},{64,128},{128,64},{192,0},{8,72},{72,8},{136,200},{200,136... | collective-permute-start | bytes 638984 | tf_op jit(solution)/shard_map/ppermute | solution.py:286
  29.3 0.0 collective-permute-done.6.g0
  29.3 1.1 %collective-permute-done.7.g1 = bf16[8,104,128]{2,1,0:T(8,128)(2,1)S(1)} collective-permute-done((bf16[8,104,128]{2,1,0:T(8,128)(2,1)S(1)}, bf16[8,104,128]{2,1,0:T(8,128)(2,1)S(1)}, u32[]{:S(2)}, u32[]{:S(2)}) %collective-permute-start.7) | collective-permute-done | bytes 213024 | tf_op jit(solution)/shard_map/ppermute | solution.py:286
  30.5 2.9 %collective-permute-done.8.g2 = bf16[8,104,128]{2,1,0:T(8,128)(2,1)S(1)} collective-permute-done((bf16[8,104,128]{2,1,0:T(8,128)(2,1)S(1)}, bf16[8,104,128]{2,1,0:T(8,128)(2,1)S(1)}, u32[]{:S(2)}, u32[]{:S(2)}) %collective-permute-start.8) | collective-permute-done | bytes 213024 | tf_op jit(solution)/shard_map/ppermute | solution.py:286
  33.4 0.3 add_four.1
  33.7 17.2 %all_to_all.10.in_ref = bf16[32,80,128]{2,1,0:T(8,128)(2,1)S(1)} all-to-all(bf16[32,80,128]{2,1,0:T(8,128)(2,1)S(1)} %add_four.1), channel_id=1, replica_groups=mesh['y'=4,'zh'=4,'c'=2,'zl'=2,'x'=4] {'y','zl','x'}, dimensions={0} | all-to-all | bytes 1310720 | tf_op jit(solution)/shard_map/all_to_all | solution.py:267
  50.8 0.1 sum_near.1
  50.9 12.5 %all_to_all.11.in_ref = bf16[4,80,128]{2,1,0:T(8,128)(2,1)S(1)} all-to-all(bf16[4,80,128]{2,1,0:T(8,128)(2,1)S(1)} %sum_near.1), channel_id=1, replica_groups=mesh['y'=4,'zh'=4,'c'=2,'zl'=2,'x'=4] {'zh'}, dimensions={0} | all-to-all | bytes 163840 | tf_op jit(solution)/shard_map/all_to_all | solution.py:267
  63.4 0.6 sum_far.1
Async XLA Ops:
  7.4 2.5 %collective-permute-start = (bf16[208,8,256]{2,1,0:T(8,128)(2,1)S(1)}, bf16[208,8,256]{2,1,0:T(8,128)(2,1)S(1)}, u32[]{:S(2)}, u32[]{:S(2)}) collective-permute-start(bf16[208,8,256]{2,1,0:T(8,128)(2,1)S(1)} %get-tuple-element.24), channel_id=1, source_target_pairs={{0,8},{8,0},{1,9},{9,1},{2,10},{10,2},{3,11},{11,3},{4,12},{12,4},... | collective-permute-start | bytes 2555912 | tf_op jit(solution)/shard_map/ppermute | solution.py:283
  7.5 4.6 %collective-permute-start.2 = (bf16[208,8,256]{2,1,0:T(8,128)(2,1)S(1)}, bf16[208,8,256]{2,1,0:T(8,128)(2,1)S(1)}, u32[]{:S(2)}, u32[]{:S(2)}) collective-permute-start(bf16[208,8,256]{2,1,0:T(8,128)(2,1)S(1)} %get-tuple-element.29), channel_id=1, source_target_pairs={{0,8},{8,0},{1,9},{9,1},{2,10},{10,2},{3,11},{11,3},{4,12},{12,4},... | collective-permute-start | bytes 2555912 | tf_op jit(solution)/shard_map/ppermute | solution.py:283
  8.0 5.7 %collective-permute-start.4 = (bf16[208,8,256]{2,1,0:T(8,128)(2,1)S(1)}, bf16[208,8,256]{2,1,0:T(8,128)(2,1)S(1)}, u32[]{:S(2)}, u32[]{:S(2)}) collective-permute-start(bf16[208,8,256]{2,1,0:T(8,128)(2,1)S(1)} %get-tuple-element.34), channel_id=1, source_target_pairs={{0,8},{8,0},{1,9},{9,1},{2,10},{10,2},{3,11},{11,3},{4,12},{12,4},... | collective-permute-start | bytes 2555912 | tf_op jit(solution)/shard_map/ppermute | solution.py:283
  10.2 8.2 %collective-permute-start.1 = (bf16[2,8,104,128]{3,2,1,0:T(8,128)(2,1)S(1)}, bf16[2,8,104,128]{3,2,1,0:T(8,128)(2,1)S(1)}, u32[]{:S(2)}, u32[]{:S(2)}) collective-permute-start(bf16[2,8,104,128]{3,2,1,0:T(8,128)(2,1)S(1)} %get-tuple-element.26), channel_id=1, source_target_pairs={{0,4},{4,0},{16,20},{20,16},{32,36},{36,32},{48,52},{52,48},{8,60}... | collective-permute-start | bytes 1277960 | tf_op jit(solution)/shard_map/ppermute | solution.py:286
  12.4 12.0 %collective-permute-start.3 = (bf16[2,8,104,128]{3,2,1,0:T(8,128)(2,1)S(1)}, bf16[2,8,104,128]{3,2,1,0:T(8,128)(2,1)S(1)}, u32[]{:S(2)}, u32[]{:S(2)}) collective-permute-start(bf16[2,8,104,128]{3,2,1,0:T(8,128)(2,1)S(1)} %get-tuple-element.31), channel_id=1, source_target_pairs={{0,1},{1,0},{2,3},{3,2},{8,11},{9,10},{10,9},{11,8},{4,5},{5,4},{6... | collective-permute-start | bytes 1277960 | tf_op jit(solution)/shard_map/ppermute | solution.py:286
  14.0 12.1 %collective-permute-start.5 = (bf16[2,8,104,128]{3,2,1,0:T(8,128)(2,1)S(1)}, bf16[2,8,104,128]{3,2,1,0:T(8,128)(2,1)S(1)}, u32[]{:S(2)}, u32[]{:S(2)}) collective-permute-start(bf16[2,8,104,128]{3,2,1,0:T(8,128)(2,1)S(1)} %get-tuple-element.36), channel_id=1, source_target_pairs={{0,64},{64,0},{128,192},{192,128},{8,200},{72,136},{136,72},{200,8... | collective-permute-start | bytes 1277960 | tf_op jit(solution)/shard_map/ppermute | solution.py:286
  18.5 10.8 %collective-permute-start.6 = (bf16[8,104,128]{2,1,0:T(8,128)(2,1)S(1)}, bf16[8,104,128]{2,1,0:T(8,128)(2,1)S(1)}, u32[]{:S(2)}, u32[]{:S(2)}) collective-permute-start(bf16[8,104,128]{2,1,0:T(8,128)(2,1)S(1)} %get-tuple-element.38), channel_id=1, source_target_pairs={{0,52},{4,16},{16,4},{20,32},{32,20},{36,48},{48,36},{52,0},{8,12}... | collective-permute-start | bytes 638984 | tf_op jit(solution)/shard_map/ppermute | solution.py:286
  24.5 5.9 %collective-permute-start.7 = (bf16[8,104,128]{2,1,0:T(8,128)(2,1)S(1)}, bf16[8,104,128]{2,1,0:T(8,128)(2,1)S(1)}, u32[]{:S(2)}, u32[]{:S(2)}) collective-permute-start(bf16[8,104,128]{2,1,0:T(8,128)(2,1)S(1)} %get-tuple-element.39), channel_id=1, source_target_pairs={{0,3},{1,2},{2,1},{3,0},{8,9},{9,8},{10,11},{11,10},{4,7},{5,6},{6... | collective-permute-start | bytes 638984 | tf_op jit(solution)/shard_map/ppermute | solution.py:286
  26.2 7.1 %collective-permute-start.8 = (bf16[8,104,128]{2,1,0:T(8,128)(2,1)S(1)}, bf16[8,104,128]{2,1,0:T(8,128)(2,1)S(1)}, u32[]{:S(2)}, u32[]{:S(2)}) collective-permute-start(bf16[8,104,128]{2,1,0:T(8,128)(2,1)S(1)} %get-tuple-element.40), channel_id=1, source_target_pairs={{0,192},{64,128},{128,64},{192,0},{8,72},{72,8},{136,200},{200,136... | collective-permute-start | bytes 638984 | tf_op jit(solution)/shard_map/ppermute | solution.py:286

commit v5 on v4

--- a/solution.py
+++ b/solution.py
@@ -19,7 +19,7 @@
 AXES = ("y", "zh", "c", "zl", "x")
 ORDER = "zxy"
 PAD = 80
-TERMS_MIB = 40
+FIRST_MIB = 28
 F32 = jnp.float32
 BF16 = jnp.bfloat16
 VM = pl.BlockSpec(memory_space=pltpu.VMEM)
@@ -42,14 +42,17 @@
             out[i, 8 * r0 : 8 * (r0 + 1), lanes] = rows[i, half, pl.ds(r0, 8, stride=NR0), :]
 
 
-def weight_grads(mine, a_ref, v_ref, sends, owns):
-    for cb in range(NCB):
-        res = jnp.dot(a_ref[...], v_ref[:, cb * BLK : (cb + 1) * BLK], preferred_element_type=F32)
-        for r0 in range(NR0):
-            quarter, off = divmod(NCB * r0 + cb, QUART)
-            for m, out in enumerate(owns if quarter % 2 == mine else sends):
-                lo = m * ROWS + 8 * r0
-                out[QUART * (quarter // 2) + off] = res[lo : lo + 8, :].astype(BF16)
+def weight_grads(a_ref, v_ref, send, own):
+    for mine in range(2):
+
+        @pl.when(lax.axis_index("c") == mine)
+        def _(mine=mine):
+            for cb in range(NCB):
+                res = jnp.dot(a_ref[...], v_ref[:, cb * BLK : (cb + 1) * BLK], preferred_element_type=F32)
+                for r0 in range(NR0):
+                    quarter, off = divmod(NCB * r0 + cb, QUART)
+                    out = own if quarter % 2 == mine else send
+                    out[QUART * (quarter // 2) + off] = res[8 * r0 : 8 * (r0 + 1), :].astype(BF16)
 
 
 def fetch(pairs, sems):
@@ -62,9 +65,8 @@
     return copies
 
 
-def terms_kernel(x_hbm, g_hbm, wg_hbm, wu_hbm, wd_hbm, *rest):
-    sends, owns, scratch = rest[0:3], rest[3:6], rest[6:]
-    x_ref, g_ref, wg_ref, wu_ref, wd_ref, rows, tmp, a0_ref, a12_ref, sems = scratch
+def first_kernel(x_hbm, g_hbm, wg_hbm, wu_hbm, wd_hbm, send, own, x_ref, a1_ref, a2_ref, *scratch):
+    g_ref, wg_ref, wu_ref, wd_ref, rows, tmp, a0_ref, sems = scratch
     pairs = ((x_hbm, x_ref), (wg_hbm, wg_ref), (wu_hbm, wu_ref), (g_hbm, g_ref), (wd_hbm, wd_ref))
     fetched = fetch(pairs, sems)
 
@@ -87,26 +89,21 @@
     permuted(act * up, rows, tmp, 0)
     permuted(dh * up * sig * (1.0 + gate * (1.0 - sig)), rows, tmp, 1)
     permuted(dh * act, rows, tmp, 2)
-    a0_ref[...] = tmp[0].astype(BF16)
-    a12_ref[...] = jnp.concatenate([tmp[1], tmp[2]], axis=0).astype(BF16)
-    for mine in range(2):
-
-        @pl.when(lax.axis_index("c") == mine)
-        def _(mine=mine):
-            weight_grads(mine, a0_ref, g_ref, sends[:1], owns[:1])
-            weight_grads(mine, a12_ref, x_ref, sends[1:], owns[1:])
-
-
-def terms(*inputs):
+    for i, out in enumerate((a0_ref, a1_ref, a2_ref)):
+        out[...] = tmp[i].astype(BF16)
+    weight_grads(a0_ref, g_ref, send, own)
+
+
+def first(*inputs):
+    inputs = [pltpu.with_memory_space_constraint(a, pltpu.HBM) for a in inputs]
     half = pltpu.VMEM((2 * QUART, 8, BLK), BF16)
-    inputs = [pltpu.with_memory_space_constraint(a, pltpu.HBM) for a in inputs]
-    return pl.pallas_call(
-        terms_kernel,
+    act = pltpu.VMEM((ROWS, TOK), BF16)
+    return pl.pallas_call(
+        first_kernel,
         in_specs=[HB] * 5,
-        out_specs=[VM] * 6,
-        out_shape=[half] * 6,
+        out_specs=[VM] * 5,
+        out_shape=[half, half, pltpu.VMEM((TOK, D), BF16), act, act],
         scratch_shapes=[
-            pltpu.VMEM((TOK, D), BF16),
             pltpu.VMEM((TOK, D), BF16),
             pltpu.VMEM((ROWS, D), BF16),
             pltpu.VMEM((ROWS, D), BF16),
@@ -114,12 +111,24 @@
             pltpu.VMEM((3, 2, ROWS, 128), F32),
             pltpu.VMEM((3, ROWS, TOK), F32),
             pltpu.VMEM((ROWS, TOK), BF16),
-            pltpu.VMEM((2 * ROWS, TOK), BF16),
             pltpu.SemaphoreType.DMA((5, len(CUTS) - 1)),
         ],
-        compiler_params=params(TERMS_MIB),
-        name="terms",
+        compiler_params=params(FIRST_MIB),
+        name="first",
     )(*inputs)
+
+
+def grads(a, v):
+    half = pltpu.VMEM((2 * QUART, 8, BLK), BF16)
+    return pl.pallas_call(
+        weight_grads,
+        in_specs=[VM] * 2,
+        out_specs=[VM] * 2,
+        out_shape=[half] * 2,
+        compiler_params=params(16),
+        cost_estimate=pl.CostEstimate(flops=2 * ROWS * TOK * D, bytes_accessed=8 * TOK * D, transcendentals=0),
+        name="grads",
+    )(a, v)
 
 
 def pair_place(axis, level):
@@ -277,9 +286,11 @@
             "z": (("zh", "c", "zl"), [(place(i, c), place(long[i][k], c)) for c, k in cores for i in range(8)]),
         }
 
-    sends_owns = terms(tokens, grad_out, gate_rows, up_rows, down_rows)
+    send, own, x_here, *acts = first(tokens, grad_out, gate_rows, up_rows, down_rows)
     keeps, gots = [], []
-    for axis, send, own in zip(ORDER, sends_owns[:3], sends_owns[3:], strict=True):
+    for m, axis in enumerate(ORDER):
+        if m:
+            send, own = grads(acts[m - 1], x_here)
         parts = add_cores(axis, own, lax.ppermute(send, "c", [(0, 1), (1, 0)]))
         for level in range(2):
             keep, give = parts if level == 0 else add_pair(axis, keep, got)

time: 64.2 us -> 63.4 us (0.988)
  waiting for transfers between devices: 9.22 us -> 7.57 us
    ppermute x3, waiting for transfers between devices: 1.77 us -> 0.11 us  [per_device(): parts = add_cores(axis, own, lax.ppermute(send, 'c', [(0, 1), (1, 0)]))]
    pallas_call x1 -> x3, Pallas kernels: 7.44 us -> 8.1 us  [the longest x1 6.54 us: first(): pl.pallas_call(first_kernel, in_specs=[HB] * 5, out_specs=[VM] * 5, out_s...]
  transfers between devices with their start and end apart: 9 -> 9, of which waited for: 4 -> 4; matrix products, arithmetic and copies ran while one was open for 0% -> 0% of each run, Pallas kernels for 2% -> 4%
where the time goes in v5:
time: 63.4 us; the launch traced here: 63.3 us
  blocking collectives  29.7 us (47%)
  starting transfers between devices  15.7 us (25%)
  Pallas kernels  10.2 us (16%)
  waiting for transfers between devices  7.57 us (12%)
    all_to_all x2, blocking collectives, exchange(): return lax.all_to_all(parts, axes, split_axis=0, concat_axis=0, tiled=True)  29.7 us
    ppermute x6, starting transfers between devices, per_device(): got = lax.ppermute(give, *pairs(level)[axis])  14.9 us
    ppermute x6, waiting for transfers between devices, per_device(): got = lax.ppermute(give, *pairs(level)[axis])  7.45 us
    pallas_call x1, Pallas kernels, first(): pl.pallas_call(first_kernel, in_specs=[HB] * 5, out_specs=[VM] * 5, out_s...  6.54 us
    pallas_call x2, Pallas kernels, grads(): pl.pallas_call(weight_grads, in_specs=[VM] * 2, out_specs=[VM] * 2, out_s...  1.56 us
  transfers between devices with their start and end apart: 9, of which 4 were waited for; matrix products, arithmetic and copies ran while one was open for 0% of the time, Pallas kernels for 4%

profile of v5, /device:TPU:2, one launch (start us, length us, event | category | flops | bytes accessed | tf_op | source)
XLA Modules:
  0.0 63.3 jit_solution(8560232149307619786)
XLA Ops:
  0.0 6.5 %first.1 = (bf16[208,8,256]{2,1,0:T(8,128)(2,1)S(1)}, bf16[208,8,256]{2,1,0:T(8,128)(2,1)S(1)}, bf16[256,8192]{1,0:T(8,128)(2,1)S(1)}, bf16[104,256]{1,0:T(8,128)(2,1)S(1)}, bf16[104,256]{1,0:T(8,128)(2,1)S(1)}) custom-call(bf16[256,8192]{1,0:T(8,128)(2,1)} %x_hbm.1, bf16[256,8192]{1,0:T(8,128)(2,1)} %g_hbm.1, bf16[104,8192]{1,0:T(8,128)(2,1)} %wg_hbm.1, ...), custom_call_target="tpu_custom_call" | custom-call | tf_op jit(solution)/shard_map/first/pallas_call | solution.py:101
  6.5 0.1 collective-permute-start
  6.6 0.8 %grads.2 = (bf16[208,8,256]{2,1,0:T(8,128)(2,1)S(1)}, bf16[208,8,256]{2,1,0:T(8,128)(2,1)S(1)}) custom-call(bf16[104,256]{1,0:T(8,128)(2,1)S(1)} %get-tuple-element.31.a_ref, bf16[256,8192]{1,0:T(8,128)(2,1)S(1)} %get-tuple-element.32.v_ref), custom_call_target="tpu_custom_call" | custom-call | flops 436207616 | bytes 16777216 | tf_op jit(solution)/shard_map/grads/pallas_call | solution.py:123
  7.4 0.6 collective-permute-start.2
  8.0 0.8 %grads.3 = (bf16[208,8,256]{2,1,0:T(8,128)(2,1)S(1)}, bf16[208,8,256]{2,1,0:T(8,128)(2,1)S(1)}) custom-call(bf16[104,256]{1,0:T(8,128)(2,1)S(1)} %get-tuple-element.38.a_ref, bf16[256,8192]{1,0:T(8,128)(2,1)S(1)} %get-tuple-element.32.v_ref), custom_call_target="tpu_custom_call" | custom-call | flops 436207616 | bytes 16777216 | tf_op jit(solution)/shard_map/grads/pallas_call | solution.py:123
  8.8 0.1 collective-permute-start.4
  8.9 0.1 collective-permute-done.got
  9.0 0.3 add_z.1
  9.3 2.0 %collective-permute-start.1 = (bf16[2,8,104,128]{3,2,1,0:T(8,128)(2,1)S(1)}, bf16[2,8,104,128]{3,2,1,0:T(8,128)(2,1)S(1)}, u32[]{:S(2)}, u32[]{:S(2)}) collective-permute-start(bf16[2,8,104,128]{3,2,1,0:T(8,128)(2,1)S(1)} %get-tuple-element.29), channel_id=1, source_target_pairs={{0,4},{4,0},{16,20},{20,16},{32,36},{36,32},{48,52},{52,48},{8,60}... | collective-permute-start | bytes 1277960 | tf_op jit(solution)/shard_map/ppermute | solution.py:297
  11.3 0.0 collective-permute-done.2.got
  11.3 0.3 add_x.1
  11.5 1.3 %collective-permute-start.3 = (bf16[2,8,104,128]{3,2,1,0:T(8,128)(2,1)S(1)}, bf16[2,8,104,128]{3,2,1,0:T(8,128)(2,1)S(1)}, u32[]{:S(2)}, u32[]{:S(2)}) collective-permute-start(bf16[2,8,104,128]{3,2,1,0:T(8,128)(2,1)S(1)} %get-tuple-element.36), channel_id=1, source_target_pairs={{0,1},{1,0},{2,3},{3,2},{8,11},{9,10},{10,9},{11,8},{4,5},{5,4},{6... | collective-permute-start | bytes 1277960 | tf_op jit(solution)/shard_map/ppermute | solution.py:297
  12.8 0.0 collective-permute-done.4.got
  12.8 0.3 add_y.1
  13.1 1.0 %collective-permute-start.5 = (bf16[2,8,104,128]{3,2,1,0:T(8,128)(2,1)S(1)}, bf16[2,8,104,128]{3,2,1,0:T(8,128)(2,1)S(1)}, u32[]{:S(2)}, u32[]{:S(2)}) collective-permute-start(bf16[2,8,104,128]{3,2,1,0:T(8,128)(2,1)S(1)} %get-tuple-element.42), channel_id=1, source_target_pairs={{0,64},{64,0},{128,192},{192,128},{8,200},{72,136},{136,72},{200,8... | collective-permute-start | bytes 1277960 | tf_op jit(solution)/shard_map/ppermute | solution.py:297
  14.1 3.4 %collective-permute-done.1.got = bf16[2,8,104,128]{3,2,1,0:T(8,128)(2,1)S(1)} collective-permute-done((bf16[2,8,104,128]{3,2,1,0:T(8,128)(2,1)S(1)}, bf16[2,8,104,128]{3,2,1,0:T(8,128)(2,1)S(1)}, u32[]{:S(2)}, u32[]{:S(2)}) %collective-permute-start.1) | collective-permute-done | bytes 426016 | tf_op jit(solution)/shard_map/ppermute | solution.py:297
  17.5 0.1 add_pair_z.1
  17.6 5.9 %collective-permute-start.6 = (bf16[8,104,128]{2,1,0:T(8,128)(2,1)S(1)}, bf16[8,104,128]{2,1,0:T(8,128)(2,1)S(1)}, u32[]{:S(2)}, u32[]{:S(2)}) collective-permute-start(bf16[8,104,128]{2,1,0:T(8,128)(2,1)S(1)} %get-tuple-element.44), channel_id=1, source_target_pairs={{0,52},{4,16},{16,4},{20,32},{32,20},{36,48},{48,36},{52,0},{8,12}... | collective-permute-start | bytes 638984 | tf_op jit(solution)/shard_map/ppermute | solution.py:297
  23.5 0.0 collective-permute-done.3.got
  23.5 0.1 add_pair_x.1
  23.6 1.6 %collective-permute-start.7 = (bf16[8,104,128]{2,1,0:T(8,128)(2,1)S(1)}, bf16[8,104,128]{2,1,0:T(8,128)(2,1)S(1)}, u32[]{:S(2)}, u32[]{:S(2)}) collective-permute-start(bf16[8,104,128]{2,1,0:T(8,128)(2,1)S(1)} %get-tuple-element.45), channel_id=1, source_target_pairs={{0,3},{1,2},{2,1},{3,0},{8,9},{9,8},{10,11},{11,10},{4,7},{5,6},{6... | collective-permute-start | bytes 638984 | tf_op jit(solution)/shard_map/ppermute | solution.py:297
  25.2 0.0 collective-permute-done.5.got
  25.2 0.1 add_pair_y.1
  25.3 3.1 %collective-permute-start.8 = (bf16[8,104,128]{2,1,0:T(8,128)(2,1)S(1)}, bf16[8,104,128]{2,1,0:T(8,128)(2,1)S(1)}, u32[]{:S(2)}, u32[]{:S(2)}) collective-permute-start(bf16[8,104,128]{2,1,0:T(8,128)(2,1)S(1)} %get-tuple-element.46), channel_id=1, source_target_pairs={{0,192},{64,128},{128,64},{192,0},{8,72},{72,8},{136,200},{200,136... | collective-permute-start | bytes 638984 | tf_op jit(solution)/shard_map/ppermute | solution.py:297
  28.4 0.0 collective-permute-done.6.g0
  28.4 1.1 %collective-permute-done.7.g1 = bf16[8,104,128]{2,1,0:T(8,128)(2,1)S(1)} collective-permute-done((bf16[8,104,128]{2,1,0:T(8,128)(2,1)S(1)}, bf16[8,104,128]{2,1,0:T(8,128)(2,1)S(1)}, u32[]{:S(2)}, u32[]{:S(2)}) %collective-permute-start.7) | collective-permute-done | bytes 213024 | tf_op jit(solution)/shard_map/ppermute | solution.py:297
  29.6 2.9 %collective-permute-done.8.g2 = bf16[8,104,128]{2,1,0:T(8,128)(2,1)S(1)} collective-permute-done((bf16[8,104,128]{2,1,0:T(8,128)(2,1)S(1)}, bf16[8,104,128]{2,1,0:T(8,128)(2,1)S(1)}, u32[]{:S(2)}, u32[]{:S(2)}) %collective-permute-start.8) | collective-permute-done | bytes 213024 | tf_op jit(solution)/shard_map/ppermute | solution.py:297
  32.5 0.3 add_four.1
  32.8 17.4 %all_to_all.10.in_ref = bf16[32,80,128]{2,1,0:T(8,128)(2,1)S(1)} all-to-all(bf16[32,80,128]{2,1,0:T(8,128)(2,1)S(1)} %add_four.1), channel_id=1, replica_groups=mesh['y'=4,'zh'=4,'c'=2,'zl'=2,'x'=4] {'y','zl','x'}, dimensions={0} | all-to-all | bytes 1310720 | tf_op jit(solution)/shard_map/all_to_all | solution.py:276
  50.2 0.1 sum_near.1
  50.3 12.3 %all_to_all.11.in_ref = bf16[4,80,128]{2,1,0:T(8,128)(2,1)S(1)} all-to-all(bf16[4,80,128]{2,1,0:T(8,128)(2,1)S(1)} %sum_near.1), channel_id=1, replica_groups=mesh['y'=4,'zh'=4,'c'=2,'zl'=2,'x'=4] {'zh'}, dimensions={0} | all-to-all | bytes 163840 | tf_op jit(solution)/shard_map/all_to_all | solution.py:276
  62.6 0.6 %sum_far.1 = f32[3,13,256]{2,1,0:T(8,128)} custom-call(bf16[4,80,128]{2,1,0:T(8,128)(2,1)S(1)} %all_to_all.11.in_ref), custom_call_target="tpu_custom_call" | custom-call | tf_op jit(solution)/shard_map/sum_far/pallas_call | solution.py:264
Async XLA Ops:
  6.5 2.5 %collective-permute-start = (bf16[208,8,256]{2,1,0:T(8,128)(2,1)S(1)}, bf16[208,8,256]{2,1,0:T(8,128)(2,1)S(1)}, u32[]{:S(2)}, u32[]{:S(2)}) collective-permute-start(bf16[208,8,256]{2,1,0:T(8,128)(2,1)S(1)} %get-tuple-element.27), channel_id=1, source_target_pairs={{0,8},{8,0},{1,9},{9,1},{2,10},{10,2},{3,11},{11,3},{4,12},{12,4},... | collective-permute-start | bytes 2555912 | tf_op jit(solution)/shard_map/ppermute | solution.py:294
  7.4 3.9 %collective-permute-start.2 = (bf16[208,8,256]{2,1,0:T(8,128)(2,1)S(1)}, bf16[208,8,256]{2,1,0:T(8,128)(2,1)S(1)}, u32[]{:S(2)}, u32[]{:S(2)}) collective-permute-start(bf16[208,8,256]{2,1,0:T(8,128)(2,1)S(1)} %get-tuple-element.34), channel_id=1, source_target_pairs={{0,8},{8,0},{1,9},{9,1},{2,10},{10,2},{3,11},{11,3},{4,12},{12,4},... | collective-permute-start | bytes 2555912 | tf_op jit(solution)/shard_map/ppermute | solution.py:294
  8.8 4.0 %collective-permute-start.4 = (bf16[208,8,256]{2,1,0:T(8,128)(2,1)S(1)}, bf16[208,8,256]{2,1,0:T(8,128)(2,1)S(1)}, u32[]{:S(2)}, u32[]{:S(2)}) collective-permute-start(bf16[208,8,256]{2,1,0:T(8,128)(2,1)S(1)} %get-tuple-element.40), channel_id=1, source_target_pairs={{0,8},{8,0},{1,9},{9,1},{2,10},{10,2},{3,11},{11,3},{4,12},{12,4},... | collective-permute-start | bytes 2555912 | tf_op jit(solution)/shard_map/ppermute | solution.py:294
  9.3 8.2 %collective-permute-start.1 = (bf16[2,8,104,128]{3,2,1,0:T(8,128)(2,1)S(1)}, bf16[2,8,104,128]{3,2,1,0:T(8,128)(2,1)S(1)}, u32[]{:S(2)}, u32[]{:S(2)}) collective-permute-start(bf16[2,8,104,128]{3,2,1,0:T(8,128)(2,1)S(1)} %get-tuple-element.29), channel_id=1, source_target_pairs={{0,4},{4,0},{16,20},{20,16},{32,36},{36,32},{48,52},{52,48},{8,60}... | collective-permute-start | bytes 1277960 | tf_op jit(solution)/shard_map/ppermute | solution.py:297
  11.5 12.0 %collective-permute-start.3 = (bf16[2,8,104,128]{3,2,1,0:T(8,128)(2,1)S(1)}, bf16[2,8,104,128]{3,2,1,0:T(8,128)(2,1)S(1)}, u32[]{:S(2)}, u32[]{:S(2)}) collective-permute-start(bf16[2,8,104,128]{3,2,1,0:T(8,128)(2,1)S(1)} %get-tuple-element.36), channel_id=1, source_target_pairs={{0,1},{1,0},{2,3},{3,2},{8,11},{9,10},{10,9},{11,8},{4,5},{5,4},{6... | collective-permute-start | bytes 1277960 | tf_op jit(solution)/shard_map/ppermute | solution.py:297
  13.1 12.1 %collective-permute-start.5 = (bf16[2,8,104,128]{3,2,1,0:T(8,128)(2,1)S(1)}, bf16[2,8,104,128]{3,2,1,0:T(8,128)(2,1)S(1)}, u32[]{:S(2)}, u32[]{:S(2)}) collective-permute-start(bf16[2,8,104,128]{3,2,1,0:T(8,128)(2,1)S(1)} %get-tuple-element.42), channel_id=1, source_target_pairs={{0,64},{64,0},{128,192},{192,128},{8,200},{72,136},{136,72},{200,8... | collective-permute-start | bytes 1277960 | tf_op jit(solution)/shard_map/ppermute | solution.py:297
  17.6 10.8 %collective-permute-start.6 = (bf16[8,104,128]{2,1,0:T(8,128)(2,1)S(1)}, bf16[8,104,128]{2,1,0:T(8,128)(2,1)S(1)}, u32[]{:S(2)}, u32[]{:S(2)}) collective-permute-start(bf16[8,104,128]{2,1,0:T(8,128)(2,1)S(1)} %get-tuple-element.44), channel_id=1, source_target_pairs={{0,52},{4,16},{16,4},{20,32},{32,20},{36,48},{48,36},{52,0},{8,12}... | collective-permute-start | bytes 638984 | tf_op jit(solution)/shard_map/ppermute | solution.py:297
  23.6 5.9 %collective-permute-start.7 = (bf16[8,104,128]{2,1,0:T(8,128)(2,1)S(1)}, bf16[8,104,128]{2,1,0:T(8,128)(2,1)S(1)}, u32[]{:S(2)}, u32[]{:S(2)}) collective-permute-start(bf16[8,104,128]{2,1,0:T(8,128)(2,1)S(1)} %get-tuple-element.45), channel_id=1, source_target_pairs={{0,3},{1,2},{2,1},{3,0},{8,9},{9,8},{10,11},{11,10},{4,7},{5,6},{6... | collective-permute-start | bytes 638984 | tf_op jit(solution)/shard_map/ppermute | solution.py:297
  25.3 7.1 %collective-permute-start.8 = (bf16[8,104,128]{2,1,0:T(8,128)(2,1)S(1)}, bf16[8,104,128]{2,1,0:T(8,128)(2,1)S(1)}, u32[]{:S(2)}, u32[]{:S(2)}) collective-permute-start(bf16[8,104,128]{2,1,0:T(8,128)(2,1)S(1)} %get-tuple-element.46), channel_id=1, source_target_pairs={{0,192},{64,128},{128,64},{192,0},{8,72},{72,8},{136,200},{200,136... | collective-permute-start | bytes 638984 | tf_op jit(solution)/shard_map/ppermute | solution.py:297

commit v6 on v5

--- a/solution.py
+++ b/solution.py
@@ -150,8 +150,8 @@
                 for half in range(2):
                     halves[half, low, d, pl.ds(off, 8, stride=OWN), :] = tile[:, 128 * half : 128 * (half + 1)]
     mine = pair_place(axis, 0)
-    keep[...] = halves[mine].astype(BF16)
-    give[...] = halves[1 - mine].astype(BF16)
+    for out, half in ((keep, mine), (give, 1 - mine)):
+        out[...] = halves[half].reshape(2, 64 * OWN, 128).astype(BF16)
 
 
 def add_cores(axis, own, got):
@@ -159,7 +159,7 @@
         functools.partial(add_kernel, axis),
         in_specs=[VM] * 2,
         out_specs=[VM] * 2,
-        out_shape=[shape(2, 8, 8 * OWN, 128)] * 2,
+        out_shape=[shape(2, 64 * OWN, 128)] * 2,
         scratch_shapes=[pltpu.VMEM((2, 2, 8, 8 * OWN, 128), F32)],
         compiler_params=params(16),
         name="add_" + axis,
@@ -177,7 +177,7 @@
         functools.partial(add_pair_kernel, axis),
         in_specs=[VM] * 2,
         out_specs=[VM] * 2,
-        out_shape=[shape(8, 8 * OWN, 128)] * 2,
+        out_shape=[shape(64 * OWN, 128)] * 2,
         compiler_params=params(16),
         name="add_pair_" + axis,
     )(mine, got)
@@ -187,7 +187,7 @@
     n = 2 * OWN
     packed[:, 3 * n :, :] = jnp.zeros((32, PAD - 3 * n, 128), F32)
     for m, (keep, got) in enumerate(((k0, g0), (k1, g1), (k2, g2))):
-        total[...] = keep[...].astype(F32) + got[...].astype(F32)
+        total[...] = (keep[...].astype(F32) + got[...].astype(F32)).reshape(8, 8 * OWN, 128)
         for d in range(8):
             for y in range(4):
                 packed[8 * y + d, n * m : n * (m + 1), :] = total[d, n * y : n * (y + 1), :]
@@ -223,13 +223,13 @@
             for i in range(4):
                 high, low = i >> 1, i & 1
                 half, part = (high, low) if core else (high ^ low, high)
-                total[mx, half, part] = add([s for s in range(32) if s % 4 == i], mx)
-                total[my, half, part] = add([s for s in range(32) if s // 8 == i], my)
-
-    total[mz] = jnp.zeros((2, 2, n, 128), F32)
+                total[mx, half, part, 0:n] = add([s for s in range(32) if s % 4 == i], mx)
+                total[my, half, part, 0:n] = add([s for s in range(32) if s // 8 == i], my)
+
+    total[mz] = jnp.zeros((2, 2, 32, 128), F32)
     for low in range(2):
         half = ((2 * lax.axis_index("zh") + low + 1 - lax.axis_index("c")) >> 1) & 1
-        total[mz, half, low] = add([s for s in range(32) if s // 4 % 2 == low], mz)
+        total[mz, half, low, 0:n] = add([s for s in range(32) if s // 4 % 2 == low], mz)
     packed[:, 6 * OWN :, :] = jnp.zeros((4, 2, 128), F32)
     for high in range(2):
         for low in range(2):
@@ -246,7 +246,7 @@
         in_specs=[VM],
         out_specs=VM,
         out_shape=shape(4, 80, 128),
-        scratch_shapes=[pltpu.VMEM((3, 2, 2, 2 * OWN, 128), F32), pltpu.VMEM((4, 80, 128), F32)],
+        scratch_shapes=[pltpu.VMEM((3, 2, 2, 32, 128), F32), pltpu.VMEM((4, 80, 128), F32)],
         compiler_params=params(8),
         name="sum_near",
     )(parts)

time: 63.4 us -> 63.4 us (level)
  no operation moved by 1% of the time
where the time goes in v6:
time: 63.4 us; the launch traced here: 63.3 us
  blocking collectives  29.7 us (47%)
  starting transfers between devices  15.7 us (25%)
  Pallas kernels  10.2 us (16%)
  waiting for transfers between devices  7.57 us (12%)
    all_to_all x2, blocking collectives, exchange(): return lax.all_to_all(parts, axes, split_axis=0, concat_axis=0, tiled=True)  29.7 us
    ppermute x6, starting transfers between devices, per_device(): got = lax.ppermute(give, *pairs(level)[axis])  14.9 us
    ppermute x6, waiting for transfers between devices, per_device(): got = lax.ppermute(give, *pairs(level)[axis])  7.45 us
    pallas_call x1, Pallas kernels, first(): pl.pallas_call(first_kernel, in_specs=[HB] * 5, out_specs=[VM] * 5, out_s...  6.54 us
    pallas_call x2, Pallas kernels, grads(): pl.pallas_call(weight_grads, in_specs=[VM] * 2, out_specs=[VM] * 2, out_s...  1.56 us
  transfers between devices with their start and end apart: 9, of which 4 were waited for; matrix products, arithmetic and copies ran while one was open for 0% of the time, Pallas kernels for 4%

profile of v6, /device:TPU:2, one launch (start us, length us, event | category | flops | bytes accessed | tf_op | source)
XLA Modules:
  0.0 63.3 jit_solution(10811248322067585362)
XLA Ops:
  0.0 6.5 %first.1 = (bf16[208,8,256]{2,1,0:T(8,128)(2,1)S(1)}, bf16[208,8,256]{2,1,0:T(8,128)(2,1)S(1)}, bf16[256,8192]{1,0:T(8,128)(2,1)S(1)}, bf16[104,256]{1,0:T(8,128)(2,1)S(1)}, bf16[104,256]{1,0:T(8,128)(2,1)S(1)}) custom-call(bf16[256,8192]{1,0:T(8,128)(2,1)} %x_hbm.1, bf16[256,8192]{1,0:T(8,128)(2,1)} %g_hbm.1, bf16[104,8192]{1,0:T(8,128)(2,1)} %wg_hbm.1, ...), custom_call_target="tpu_custom_call" | custom-call | tf_op jit(solution)/shard_map/first/pallas_call | solution.py:101
  6.5 0.1 collective-permute-start
  6.6 0.8 %grads.2 = (bf16[208,8,256]{2,1,0:T(8,128)(2,1)S(1)}, bf16[208,8,256]{2,1,0:T(8,128)(2,1)S(1)}) custom-call(bf16[104,256]{1,0:T(8,128)(2,1)S(1)} %get-tuple-element.31.a_ref, bf16[256,8192]{1,0:T(8,128)(2,1)S(1)} %get-tuple-element.32.v_ref), custom_call_target="tpu_custom_call" | custom-call | flops 436207616 | bytes 16777216 | tf_op jit(solution)/shard_map/grads/pallas_call | solution.py:123
  7.4 0.6 collective-permute-start.2
  8.0 0.8 %grads.3 = (bf16[208,8,256]{2,1,0:T(8,128)(2,1)S(1)}, bf16[208,8,256]{2,1,0:T(8,128)(2,1)S(1)}) custom-call(bf16[104,256]{1,0:T(8,128)(2,1)S(1)} %get-tuple-element.38.a_ref, bf16[256,8192]{1,0:T(8,128)(2,1)S(1)} %get-tuple-element.32.v_ref), custom_call_target="tpu_custom_call" | custom-call | flops 436207616 | bytes 16777216 | tf_op jit(solution)/shard_map/grads/pallas_call | solution.py:123
  8.8 0.1 collective-permute-start.4
  8.9 0.1 collective-permute-done.got
  9.0 0.3 add_z.1
  9.3 2.0 %collective-permute-start.1 = (bf16[2,832,128]{2,1,0:T(8,128)(2,1)S(1)}, bf16[2,832,128]{2,1,0:T(8,128)(2,1)S(1)}, u32[]{:S(2)}, u32[]{:S(2)}) collective-permute-start(bf16[2,832,128]{2,1,0:T(8,128)(2,1)S(1)} %get-tuple-element.29), channel_id=1, source_target_pairs={{0,4},{4,0},{16,20},{20,16},{32,36},{36,32},{48,52},{52,48},{8,60}... | collective-permute-start | bytes 1277960 | tf_op jit(solution)/shard_map/ppermute | solution.py:297
  11.3 0.0 collective-permute-done.2.got
  11.3 0.3 add_x.1
  11.5 1.3 %collective-permute-start.3 = (bf16[2,832,128]{2,1,0:T(8,128)(2,1)S(1)}, bf16[2,832,128]{2,1,0:T(8,128)(2,1)S(1)}, u32[]{:S(2)}, u32[]{:S(2)}) collective-permute-start(bf16[2,832,128]{2,1,0:T(8,128)(2,1)S(1)} %get-tuple-element.36), channel_id=1, source_target_pairs={{0,1},{1,0},{2,3},{3,2},{8,11},{9,10},{10,9},{11,8},{4,5},{5,4},{6... | collective-permute-start | bytes 1277960 | tf_op jit(solution)/shard_map/ppermute | solution.py:297
  12.8 0.0 collective-permute-done.4.got
  12.8 0.3 add_y.1
  13.1 1.0 %collective-permute-start.5 = (bf16[2,832,128]{2,1,0:T(8,128)(2,1)S(1)}, bf16[2,832,128]{2,1,0:T(8,128)(2,1)S(1)}, u32[]{:S(2)}, u32[]{:S(2)}) collective-permute-start(bf16[2,832,128]{2,1,0:T(8,128)(2,1)S(1)} %get-tuple-element.42), channel_id=1, source_target_pairs={{0,64},{64,0},{128,192},{192,128},{8,200},{72,136},{136,72},{200,8... | collective-permute-start | bytes 1277960 | tf_op jit(solution)/shard_map/ppermute | solution.py:297
  14.1 3.4 %collective-permute-done.1.got = bf16[2,832,128]{2,1,0:T(8,128)(2,1)S(1)} collective-permute-done((bf16[2,832,128]{2,1,0:T(8,128)(2,1)S(1)}, bf16[2,832,128]{2,1,0:T(8,128)(2,1)S(1)}, u32[]{:S(2)}, u32[]{:S(2)}) %collective-permute-start.1) | collective-permute-done | bytes 426016 | tf_op jit(solution)/shard_map/ppermute | solution.py:297
  17.5 0.1 add_pair_z.1
  17.6 5.9 %collective-permute-start.6 = (bf16[832,128]{1,0:T(8,128)(2,1)S(1)}, bf16[832,128]{1,0:T(8,128)(2,1)S(1)}, u32[]{:S(2)}, u32[]{:S(2)}) collective-permute-start(bf16[832,128]{1,0:T(8,128)(2,1)S(1)} %get-tuple-element.44), channel_id=1, source_target_pairs={{0,52},{4,16},{16,4},{20,32},{32,20},{36,48},{48,36},{52,0},{8,12}... | collective-permute-start | bytes 638984 | tf_op jit(solution)/shard_map/ppermute | solution.py:297
  23.5 0.0 collective-permute-done.3.got
  23.5 0.1 add_pair_x.1
  23.6 1.6 %collective-permute-start.7 = (bf16[832,128]{1,0:T(8,128)(2,1)S(1)}, bf16[832,128]{1,0:T(8,128)(2,1)S(1)}, u32[]{:S(2)}, u32[]{:S(2)}) collective-permute-start(bf16[832,128]{1,0:T(8,128)(2,1)S(1)} %get-tuple-element.45), channel_id=1, source_target_pairs={{0,3},{1,2},{2,1},{3,0},{8,9},{9,8},{10,11},{11,10},{4,7},{5,6},{6... | collective-permute-start | bytes 638984 | tf_op jit(solution)/shard_map/ppermute | solution.py:297
  25.2 0.0 collective-permute-done.5.got
  25.2 0.1 add_pair_y.1
  25.3 3.1 %collective-permute-start.8 = (bf16[832,128]{1,0:T(8,128)(2,1)S(1)}, bf16[832,128]{1,0:T(8,128)(2,1)S(1)}, u32[]{:S(2)}, u32[]{:S(2)}) collective-permute-start(bf16[832,128]{1,0:T(8,128)(2,1)S(1)} %get-tuple-element.46), channel_id=1, source_target_pairs={{0,192},{64,128},{128,64},{192,0},{8,72},{72,8},{136,200},{200,136... | collective-permute-start | bytes 638984 | tf_op jit(solution)/shard_map/ppermute | solution.py:297
  28.4 0.0 collective-permute-done.6.g0
  28.4 1.1 %collective-permute-done.7.g1 = bf16[832,128]{1,0:T(8,128)(2,1)S(1)} collective-permute-done((bf16[832,128]{1,0:T(8,128)(2,1)S(1)}, bf16[832,128]{1,0:T(8,128)(2,1)S(1)}, u32[]{:S(2)}, u32[]{:S(2)}) %collective-permute-start.7) | collective-permute-done | bytes 213024 | tf_op jit(solution)/shard_map/ppermute | solution.py:297
  29.6 2.9 %collective-permute-done.8.g2 = bf16[832,128]{1,0:T(8,128)(2,1)S(1)} collective-permute-done((bf16[832,128]{1,0:T(8,128)(2,1)S(1)}, bf16[832,128]{1,0:T(8,128)(2,1)S(1)}, u32[]{:S(2)}, u32[]{:S(2)}) %collective-permute-start.8) | collective-permute-done | bytes 213024 | tf_op jit(solution)/shard_map/ppermute | solution.py:297
  32.5 0.3 add_four.1
  32.8 17.4 %all_to_all.10.in_ref = bf16[32,80,128]{2,1,0:T(8,128)(2,1)S(1)} all-to-all(bf16[32,80,128]{2,1,0:T(8,128)(2,1)S(1)} %add_four.1), channel_id=1, replica_groups=mesh['y'=4,'zh'=4,'c'=2,'zl'=2,'x'=4] {'y','zl','x'}, dimensions={0} | all-to-all | bytes 1310720 | tf_op jit(solution)/shard_map/all_to_all | solution.py:276
  50.2 0.1 sum_near.1
  50.3 12.3 %all_to_all.11.in_ref = bf16[4,80,128]{2,1,0:T(8,128)(2,1)S(1)} all-to-all(bf16[4,80,128]{2,1,0:T(8,128)(2,1)S(1)} %sum_near.1), channel_id=1, replica_groups=mesh['y'=4,'zh'=4,'c'=2,'zl'=2,'x'=4] {'zh'}, dimensions={0} | all-to-all | bytes 163840 | tf_op jit(solution)/shard_map/all_to_all | solution.py:276
  62.6 0.6 %sum_far.1 = f32[3,13,256]{2,1,0:T(8,128)} custom-call(bf16[4,80,128]{2,1,0:T(8,128)(2,1)S(1)} %all_to_all.11.in_ref), custom_call_target="tpu_custom_call" | custom-call | tf_op jit(solution)/shard_map/sum_far/pallas_call | solution.py:264
Async XLA Ops:
  6.5 2.5 %collective-permute-start = (bf16[208,8,256]{2,1,0:T(8,128)(2,1)S(1)}, bf16[208,8,256]{2,1,0:T(8,128)(2,1)S(1)}, u32[]{:S(2)}, u32[]{:S(2)}) collective-permute-start(bf16[208,8,256]{2,1,0:T(8,128)(2,1)S(1)} %get-tuple-element.27), channel_id=1, source_target_pairs={{0,8},{8,0},{1,9},{9,1},{2,10},{10,2},{3,11},{11,3},{4,12},{12,4},... | collective-permute-start | bytes 2555912 | tf_op jit(solution)/shard_map/ppermute | solution.py:294
  7.4 3.9 %collective-permute-start.2 = (bf16[208,8,256]{2,1,0:T(8,128)(2,1)S(1)}, bf16[208,8,256]{2,1,0:T(8,128)(2,1)S(1)}, u32[]{:S(2)}, u32[]{:S(2)}) collective-permute-start(bf16[208,8,256]{2,1,0:T(8,128)(2,1)S(1)} %get-tuple-element.34), channel_id=1, source_target_pairs={{0,8},{8,0},{1,9},{9,1},{2,10},{10,2},{3,11},{11,3},{4,12},{12,4},... | collective-permute-start | bytes 2555912 | tf_op jit(solution)/shard_map/ppermute | solution.py:294
  8.8 4.0 %collective-permute-start.4 = (bf16[208,8,256]{2,1,0:T(8,128)(2,1)S(1)}, bf16[208,8,256]{2,1,0:T(8,128)(2,1)S(1)}, u32[]{:S(2)}, u32[]{:S(2)}) collective-permute-start(bf16[208,8,256]{2,1,0:T(8,128)(2,1)S(1)} %get-tuple-element.40), channel_id=1, source_target_pairs={{0,8},{8,0},{1,9},{9,1},{2,10},{10,2},{3,11},{11,3},{4,12},{12,4},... | collective-permute-start | bytes 2555912 | tf_op jit(solution)/shard_map/ppermute | solution.py:294
  9.3 8.2 %collective-permute-start.1 = (bf16[2,832,128]{2,1,0:T(8,128)(2,1)S(1)}, bf16[2,832,128]{2,1,0:T(8,128)(2,1)S(1)}, u32[]{:S(2)}, u32[]{:S(2)}) collective-permute-start(bf16[2,832,128]{2,1,0:T(8,128)(2,1)S(1)} %get-tuple-element.29), channel_id=1, source_target_pairs={{0,4},{4,0},{16,20},{20,16},{32,36},{36,32},{48,52},{52,48},{8,60}... | collective-permute-start | bytes 1277960 | tf_op jit(solution)/shard_map/ppermute | solution.py:297
  11.5 12.0 %collective-permute-start.3 = (bf16[2,832,128]{2,1,0:T(8,128)(2,1)S(1)}, bf16[2,832,128]{2,1,0:T(8,128)(2,1)S(1)}, u32[]{:S(2)}, u32[]{:S(2)}) collective-permute-start(bf16[2,832,128]{2,1,0:T(8,128)(2,1)S(1)} %get-tuple-element.36), channel_id=1, source_target_pairs={{0,1},{1,0},{2,3},{3,2},{8,11},{9,10},{10,9},{11,8},{4,5},{5,4},{6... | collective-permute-start | bytes 1277960 | tf_op jit(solution)/shard_map/ppermute | solution.py:297
  13.1 12.1 %collective-permute-start.5 = (bf16[2,832,128]{2,1,0:T(8,128)(2,1)S(1)}, bf16[2,832,128]{2,1,0:T(8,128)(2,1)S(1)}, u32[]{:S(2)}, u32[]{:S(2)}) collective-permute-start(bf16[2,832,128]{2,1,0:T(8,128)(2,1)S(1)} %get-tuple-element.42), channel_id=1, source_target_pairs={{0,64},{64,0},{128,192},{192,128},{8,200},{72,136},{136,72},{200,8... | collective-permute-start | bytes 1277960 | tf_op jit(solution)/shard_map/ppermute | solution.py:297
  17.6 10.8 %collective-permute-start.6 = (bf16[832,128]{1,0:T(8,128)(2,1)S(1)}, bf16[832,128]{1,0:T(8,128)(2,1)S(1)}, u32[]{:S(2)}, u32[]{:S(2)}) collective-permute-start(bf16[832,128]{1,0:T(8,128)(2,1)S(1)} %get-tuple-element.44), channel_id=1, source_target_pairs={{0,52},{4,16},{16,4},{20,32},{32,20},{36,48},{48,36},{52,0},{8,12}... | collective-permute-start | bytes 638984 | tf_op jit(solution)/shard_map/ppermute | solution.py:297
  23.6 5.9 %collective-permute-start.7 = (bf16[832,128]{1,0:T(8,128)(2,1)S(1)}, bf16[832,128]{1,0:T(8,128)(2,1)S(1)}, u32[]{:S(2)}, u32[]{:S(2)}) collective-permute-start(bf16[832,128]{1,0:T(8,128)(2,1)S(1)} %get-tuple-element.45), channel_id=1, source_target_pairs={{0,3},{1,2},{2,1},{3,0},{8,9},{9,8},{10,11},{11,10},{4,7},{5,6},{6... | collective-permute-start | bytes 638984 | tf_op jit(solution)/shard_map/ppermute | solution.py:297
  25.3 7.1 %collective-permute-start.8 = (bf16[832,128]{1,0:T(8,128)(2,1)S(1)}, bf16[832,128]{1,0:T(8,128)(2,1)S(1)}, u32[]{:S(2)}, u32[]{:S(2)}) collective-permute-start(bf16[832,128]{1,0:T(8,128)(2,1)S(1)} %get-tuple-element.46), channel_id=1, source_target_pairs={{0,192},{64,128},{128,64},{192,0},{8,72},{72,8},{136,200},{200,136... | collective-permute-start | bytes 638984 | tf_op jit(solution)/shard_map/ppermute | solution.py:297

commit v7 on v6

--- a/solution.py
+++ b/solution.py
@@ -76,11 +76,14 @@
     gate_up = jnp.zeros((TOK, 2 * ROWS), F32)
     dh = jnp.zeros((TOK, ROWS), F32)
     for copies, lo, hi in zip(fetched, CUTS, CUTS[1:]):
-        for copy in copies:
+        early = 3 if hi == D else 5
+        for copy in copies[:early]:
             copy.wait()
         cols = slice(lo, hi)
         both = jnp.concatenate([wg_ref[:, cols], wu_ref[:, cols]], axis=0)
         gate_up = gate_up + project(x_ref[:, cols], both)
+        for copy in copies[early:]:
+            copy.wait()
         dh = dh + project(g_ref[:, cols], wd_ref[:, cols])
     gate_up = gate_up.T
     gate, up, dh = gate_up[:ROWS], gate_up[ROWS:], dh.T

time: 63.4 us -> 63.7 us (level)
  no operation moved by 1% of the time
where the time goes in v7:
time: 63.7 us; the launch traced here: 63.5 us
  blocking collectives  29.7 us (47%)
  starting transfers between devices  15.7 us (25%)
  Pallas kernels  10.5 us (16%)
  waiting for transfers between devices  7.57 us (12%)
    all_to_all x2, blocking collectives, exchange(): return lax.all_to_all(parts, axes, split_axis=0, concat_axis=0, tiled=True)  29.7 us
    ppermute x6, starting transfers between devices, per_device(): got = lax.ppermute(give, *pairs(level)[axis])  14.9 us
    ppermute x6, waiting for transfers between devices, per_device(): got = lax.ppermute(give, *pairs(level)[axis])  7.46 us
    pallas_call x1, Pallas kernels, first(): pl.pallas_call(first_kernel, in_specs=[HB] * 5, out_specs=[VM] * 5, out_s...  6.78 us
    pallas_call x2, Pallas kernels, grads(): pl.pallas_call(weight_grads, in_specs=[VM] * 2, out_specs=[VM] * 2, out_s...  1.57 us
  transfers between devices with their start and end apart: 9, of which 4 were waited for; matrix products, arithmetic and copies ran while one was open for 0% of the time, Pallas kernels for 4%

profile of v7, /device:TPU:2, one launch (start us, length us, event | category | flops | bytes accessed | tf_op | source)
XLA Modules:
  0.0 63.5 jit_solution(11998873586877242255)
XLA Ops:
  0.0 6.8 %first.1 = (bf16[208,8,256]{2,1,0:T(8,128)(2,1)S(1)}, bf16[208,8,256]{2,1,0:T(8,128)(2,1)S(1)}, bf16[256,8192]{1,0:T(8,128)(2,1)S(1)}, bf16[104,256]{1,0:T(8,128)(2,1)S(1)}, bf16[104,256]{1,0:T(8,128)(2,1)S(1)}) custom-call(bf16[256,8192]{1,0:T(8,128)(2,1)} %x_hbm.1, bf16[256,8192]{1,0:T(8,128)(2,1)} %g_hbm.1, bf16[104,8192]{1,0:T(8,128)(2,1)} %wg_hbm.1, ...), custom_call_target="tpu_custom_call" | custom-call | tf_op jit(solution)/shard_map/first/pallas_call | solution.py:104
  6.8 0.1 collective-permute-start
  6.9 0.8 %grads.2 = (bf16[208,8,256]{2,1,0:T(8,128)(2,1)S(1)}, bf16[208,8,256]{2,1,0:T(8,128)(2,1)S(1)}) custom-call(bf16[104,256]{1,0:T(8,128)(2,1)S(1)} %get-tuple-element.31.a_ref, bf16[256,8192]{1,0:T(8,128)(2,1)S(1)} %get-tuple-element.32.v_ref), custom_call_target="tpu_custom_call" | custom-call | flops 436207616 | bytes 16777216 | tf_op jit(solution)/shard_map/grads/pallas_call | solution.py:126
  7.7 0.6 collective-permute-start.2
  8.2 0.8 %grads.3 = (bf16[208,8,256]{2,1,0:T(8,128)(2,1)S(1)}, bf16[208,8,256]{2,1,0:T(8,128)(2,1)S(1)}) custom-call(bf16[104,256]{1,0:T(8,128)(2,1)S(1)} %get-tuple-element.38.a_ref, bf16[256,8192]{1,0:T(8,128)(2,1)S(1)} %get-tuple-element.32.v_ref), custom_call_target="tpu_custom_call" | custom-call | flops 436207616 | bytes 16777216 | tf_op jit(solution)/shard_map/grads/pallas_call | solution.py:126
  9.0 0.1 collective-permute-start.4
  9.2 0.1 collective-permute-done.got
  9.3 0.3 add_z.1
  9.5 2.0 %collective-permute-start.1 = (bf16[2,832,128]{2,1,0:T(8,128)(2,1)S(1)}, bf16[2,832,128]{2,1,0:T(8,128)(2,1)S(1)}, u32[]{:S(2)}, u32[]{:S(2)}) collective-permute-start(bf16[2,832,128]{2,1,0:T(8,128)(2,1)S(1)} %get-tuple-element.29), channel_id=1, source_target_pairs={{0,4},{4,0},{16,20},{20,16},{32,36},{36,32},{48,52},{52,48},{8,60}... | collective-permute-start | bytes 1277960 | tf_op jit(solution)/shard_map/ppermute | solution.py:300
  11.5 0.0 collective-permute-done.2.got
  11.5 0.3 add_x.1
  11.8 1.3 %collective-permute-start.3 = (bf16[2,832,128]{2,1,0:T(8,128)(2,1)S(1)}, bf16[2,832,128]{2,1,0:T(8,128)(2,1)S(1)}, u32[]{:S(2)}, u32[]{:S(2)}) collective-permute-start(bf16[2,832,128]{2,1,0:T(8,128)(2,1)S(1)} %get-tuple-element.36), channel_id=1, source_target_pairs={{0,1},{1,0},{2,3},{3,2},{8,11},{9,10},{10,9},{11,8},{4,5},{5,4},{6... | collective-permute-start | bytes 1277960 | tf_op jit(solution)/shard_map/ppermute | solution.py:300
  13.1 0.0 collective-permute-done.4.got
  13.1 0.3 add_y.1
  13.3 1.0 %collective-permute-start.5 = (bf16[2,832,128]{2,1,0:T(8,128)(2,1)S(1)}, bf16[2,832,128]{2,1,0:T(8,128)(2,1)S(1)}, u32[]{:S(2)}, u32[]{:S(2)}) collective-permute-start(bf16[2,832,128]{2,1,0:T(8,128)(2,1)S(1)} %get-tuple-element.42), channel_id=1, source_target_pairs={{0,64},{64,0},{128,192},{192,128},{8,200},{72,136},{136,72},{200,8... | collective-permute-start | bytes 1277960 | tf_op jit(solution)/shard_map/ppermute | solution.py:300
  14.3 3.4 %collective-permute-done.1.got = bf16[2,832,128]{2,1,0:T(8,128)(2,1)S(1)} collective-permute-done((bf16[2,832,128]{2,1,0:T(8,128)(2,1)S(1)}, bf16[2,832,128]{2,1,0:T(8,128)(2,1)S(1)}, u32[]{:S(2)}, u32[]{:S(2)}) %collective-permute-start.1) | collective-permute-done | bytes 426016 | tf_op jit(solution)/shard_map/ppermute | solution.py:300
  17.7 0.1 add_pair_z.1
  17.8 5.9 %collective-permute-start.6 = (bf16[832,128]{1,0:T(8,128)(2,1)S(1)}, bf16[832,128]{1,0:T(8,128)(2,1)S(1)}, u32[]{:S(2)}, u32[]{:S(2)}) collective-permute-start(bf16[832,128]{1,0:T(8,128)(2,1)S(1)} %get-tuple-element.44), channel_id=1, source_target_pairs={{0,52},{4,16},{16,4},{20,32},{32,20},{36,48},{48,36},{52,0},{8,12}... | collective-permute-start | bytes 638984 | tf_op jit(solution)/shard_map/ppermute | solution.py:300
  23.8 0.0 collective-permute-done.3.got
  23.8 0.1 add_pair_x.1
  23.9 1.6 %collective-permute-start.7 = (bf16[832,128]{1,0:T(8,128)(2,1)S(1)}, bf16[832,128]{1,0:T(8,128)(2,1)S(1)}, u32[]{:S(2)}, u32[]{:S(2)}) collective-permute-start(bf16[832,128]{1,0:T(8,128)(2,1)S(1)} %get-tuple-element.45), channel_id=1, source_target_pairs={{0,3},{1,2},{2,1},{3,0},{8,9},{9,8},{10,11},{11,10},{4,7},{5,6},{6... | collective-permute-start | bytes 638984 | tf_op jit(solution)/shard_map/ppermute | solution.py:300
  25.5 0.0 collective-permute-done.5.got
  25.5 0.1 add_pair_y.1
  25.6 3.1 %collective-permute-start.8 = (bf16[832,128]{1,0:T(8,128)(2,1)S(1)}, bf16[832,128]{1,0:T(8,128)(2,1)S(1)}, u32[]{:S(2)}, u32[]{:S(2)}) collective-permute-start(bf16[832,128]{1,0:T(8,128)(2,1)S(1)} %get-tuple-element.46), channel_id=1, source_target_pairs={{0,192},{64,128},{128,64},{192,0},{8,72},{72,8},{136,200},{200,136... | collective-permute-start | bytes 638984 | tf_op jit(solution)/shard_map/ppermute | solution.py:300
  28.7 0.0 collective-permute-done.6.g0
  28.7 1.1 %collective-permute-done.7.g1 = bf16[832,128]{1,0:T(8,128)(2,1)S(1)} collective-permute-done((bf16[832,128]{1,0:T(8,128)(2,1)S(1)}, bf16[832,128]{1,0:T(8,128)(2,1)S(1)}, u32[]{:S(2)}, u32[]{:S(2)}) %collective-permute-start.7) | collective-permute-done | bytes 213024 | tf_op jit(solution)/shard_map/ppermute | solution.py:300
  29.8 2.9 %collective-permute-done.8.g2 = bf16[832,128]{1,0:T(8,128)(2,1)S(1)} collective-permute-done((bf16[832,128]{1,0:T(8,128)(2,1)S(1)}, bf16[832,128]{1,0:T(8,128)(2,1)S(1)}, u32[]{:S(2)}, u32[]{:S(2)}) %collective-permute-start.8) | collective-permute-done | bytes 213024 | tf_op jit(solution)/shard_map/ppermute | solution.py:300
  32.7 0.3 add_four.1
  33.0 17.4 %all_to_all.10.in_ref = bf16[32,80,128]{2,1,0:T(8,128)(2,1)S(1)} all-to-all(bf16[32,80,128]{2,1,0:T(8,128)(2,1)S(1)} %add_four.1), channel_id=1, replica_groups=mesh['y'=4,'zh'=4,'c'=2,'zl'=2,'x'=4] {'y','zl','x'}, dimensions={0} | all-to-all | bytes 1310720 | tf_op jit(solution)/shard_map/all_to_all | solution.py:279
  50.4 0.1 sum_near.1
  50.6 12.3 %all_to_all.11.in_ref = bf16[4,80,128]{2,1,0:T(8,128)(2,1)S(1)} all-to-all(bf16[4,80,128]{2,1,0:T(8,128)(2,1)S(1)} %sum_near.1), channel_id=1, replica_groups=mesh['y'=4,'zh'=4,'c'=2,'zl'=2,'x'=4] {'zh'}, dimensions={0} | all-to-all | bytes 163840 | tf_op jit(solution)/shard_map/all_to_all | solution.py:279
  62.9 0.6 %sum_far.1 = f32[3,13,256]{2,1,0:T(8,128)} custom-call(bf16[4,80,128]{2,1,0:T(8,128)(2,1)S(1)} %all_to_all.11.in_ref), custom_call_target="tpu_custom_call" | custom-call | tf_op jit(solution)/shard_map/sum_far/pallas_call | solution.py:267
Async XLA Ops:
  6.8 2.5 %collective-permute-start = (bf16[208,8,256]{2,1,0:T(8,128)(2,1)S(1)}, bf16[208,8,256]{2,1,0:T(8,128)(2,1)S(1)}, u32[]{:S(2)}, u32[]{:S(2)}) collective-permute-start(bf16[208,8,256]{2,1,0:T(8,128)(2,1)S(1)} %get-tuple-element.27), channel_id=1, source_target_pairs={{0,8},{8,0},{1,9},{9,1},{2,10},{10,2},{3,11},{11,3},{4,12},{12,4},... | collective-permute-start | bytes 2555912 | tf_op jit(solution)/shard_map/ppermute | solution.py:297
  7.7 3.9 %collective-permute-start.2 = (bf16[208,8,256]{2,1,0:T(8,128)(2,1)S(1)}, bf16[208,8,256]{2,1,0:T(8,128)(2,1)S(1)}, u32[]{:S(2)}, u32[]{:S(2)}) collective-permute-start(bf16[208,8,256]{2,1,0:T(8,128)(2,1)S(1)} %get-tuple-element.34), channel_id=1, source_target_pairs={{0,8},{8,0},{1,9},{9,1},{2,10},{10,2},{3,11},{11,3},{4,12},{12,4},... | collective-permute-start | bytes 2555912 | tf_op jit(solution)/shard_map/ppermute | solution.py:297
  9.0 4.0 %collective-permute-start.4 = (bf16[208,8,256]{2,1,0:T(8,128)(2,1)S(1)}, bf16[208,8,256]{2,1,0:T(8,128)(2,1)S(1)}, u32[]{:S(2)}, u32[]{:S(2)}) collective-permute-start(bf16[208,8,256]{2,1,0:T(8,128)(2,1)S(1)} %get-tuple-element.40), channel_id=1, source_target_pairs={{0,8},{8,0},{1,9},{9,1},{2,10},{10,2},{3,11},{11,3},{4,12},{12,4},... | collective-permute-start | bytes 2555912 | tf_op jit(solution)/shard_map/ppermute | solution.py:297
  9.5 8.2 %collective-permute-start.1 = (bf16[2,832,128]{2,1,0:T(8,128)(2,1)S(1)}, bf16[2,832,128]{2,1,0:T(8,128)(2,1)S(1)}, u32[]{:S(2)}, u32[]{:S(2)}) collective-permute-start(bf16[2,832,128]{2,1,0:T(8,128)(2,1)S(1)} %get-tuple-element.29), channel_id=1, source_target_pairs={{0,4},{4,0},{16,20},{20,16},{32,36},{36,32},{48,52},{52,48},{8,60}... | collective-permute-start | bytes 1277960 | tf_op jit(solution)/shard_map/ppermute | solution.py:300
  11.8 12.0 %collective-permute-start.3 = (bf16[2,832,128]{2,1,0:T(8,128)(2,1)S(1)}, bf16[2,832,128]{2,1,0:T(8,128)(2,1)S(1)}, u32[]{:S(2)}, u32[]{:S(2)}) collective-permute-start(bf16[2,832,128]{2,1,0:T(8,128)(2,1)S(1)} %get-tuple-element.36), channel_id=1, source_target_pairs={{0,1},{1,0},{2,3},{3,2},{8,11},{9,10},{10,9},{11,8},{4,5},{5,4},{6... | collective-permute-start | bytes 1277960 | tf_op jit(solution)/shard_map/ppermute | solution.py:300
  13.3 12.1 %collective-permute-start.5 = (bf16[2,832,128]{2,1,0:T(8,128)(2,1)S(1)}, bf16[2,832,128]{2,1,0:T(8,128)(2,1)S(1)}, u32[]{:S(2)}, u32[]{:S(2)}) collective-permute-start(bf16[2,832,128]{2,1,0:T(8,128)(2,1)S(1)} %get-tuple-element.42), channel_id=1, source_target_pairs={{0,64},{64,0},{128,192},{192,128},{8,200},{72,136},{136,72},{200,8... | collective-permute-start | bytes 1277960 | tf_op jit(solution)/shard_map/ppermute | solution.py:300
  17.8 10.8 %collective-permute-start.6 = (bf16[832,128]{1,0:T(8,128)(2,1)S(1)}, bf16[832,128]{1,0:T(8,128)(2,1)S(1)}, u32[]{:S(2)}, u32[]{:S(2)}) collective-permute-start(bf16[832,128]{1,0:T(8,128)(2,1)S(1)} %get-tuple-element.44), channel_id=1, source_target_pairs={{0,52},{4,16},{16,4},{20,32},{32,20},{36,48},{48,36},{52,0},{8,12}... | collective-permute-start | bytes 638984 | tf_op jit(solution)/shard_map/ppermute | solution.py:300
  23.9 5.9 %collective-permute-start.7 = (bf16[832,128]{1,0:T(8,128)(2,1)S(1)}, bf16[832,128]{1,0:T(8,128)(2,1)S(1)}, u32[]{:S(2)}, u32[]{:S(2)}) collective-permute-start(bf16[832,128]{1,0:T(8,128)(2,1)S(1)} %get-tuple-element.45), channel_id=1, source_target_pairs={{0,3},{1,2},{2,1},{3,0},{8,9},{9,8},{10,11},{11,10},{4,7},{5,6},{6... | collective-permute-start | bytes 638984 | tf_op jit(solution)/shard_map/ppermute | solution.py:300
  25.6 7.1 %collective-permute-start.8 = (bf16[832,128]{1,0:T(8,128)(2,1)S(1)}, bf16[832,128]{1,0:T(8,128)(2,1)S(1)}, u32[]{:S(2)}, u32[]{:S(2)}) collective-permute-start(bf16[832,128]{1,0:T(8,128)(2,1)S(1)} %get-tuple-element.46), channel_id=1, source_target_pairs={{0,192},{64,128},{128,64},{192,0},{8,72},{72,8},{136,200},{200,136... | collective-permute-start | bytes 638984 | tf_op jit(solution)/shard_map/ppermute | solution.py:300
